TPU v7x, 32 devices: a whole 2x2x4 slice. The times are simulated.
32 devices in a mesh: kf: 4 (over z), lat: 8 (over y, x, core).
Axes of the slice: x: 2, y: 2, z: 4, core: 2. Of those that a mesh axis runs over, the one named last changes fastest.
Arguments:
- tokens: bfloat16 [4, 4096, 256], P('kf', 'lat'), may hold values from -6 to 6
- frame_ids: int32 [4, 4096], P('kf', 'lat'), may hold values from 0 to 31, as said below
- episodes: int32 [4, 32], P('kf'), may hold values from 0 to 10
- master: float32 [5619712], P('lat'), may hold values from -8 to 8
- moment_one: float32 [5619712], P('lat'), may hold values from -6 to 6
- moment_two: float32 [5619712], P('lat'), may hold values from 0.0001 to 0.003
- latent_grad: bfloat16 [4, 32, 512, 512], P('kf', None, 'lat'), may hold values from -6 to 6
Outputs:
- latents_out: bfloat16 [4, 32, 512, 512], P('kf', None, 'lat')
- token_grad: bfloat16 [4, 4096, 256], P('kf', 'lat')
- param_grad: float32 [5619712], P('lat')
- lamb_update: float32 [5619712], P('lat')
- new_moment_one: float32 [5619712], P('lat')
- new_moment_two: float32 [5619712], P('lat')
- trust: float32 [13], replicated
- bias_grad: float32 [2, 2048], replicated
Inputs may be any that keep to these rules, and one draw needn't show every extreme that they name: `frame_ids`: every keyframe has 1 to 512 tokens in its group; in each group, exactly four keyframes have 512 tokens.
All inputs are finite; a program needn't handle non-finite values.
Results may differ from a plain program's by a relative error of at most 0.017.
Values may be sent and summed in bfloat16 or wider, within the bound.
A program may use at most 320 MiB of HBM per device.

v0:
```python
import math

import jax
import jax.numpy as jnp
from jax import lax
from jax.sharding import PartitionSpec as P

DIN = 256
D = 512
LAT = 512
CH = 64
HEADS = 8
HEAD_DIM = 64
FF = 2048
EPISODES = 11
NPARAM = 5619712


norm_eps = 1e-05
masked_fill = -1e30
beta_one = 0.9
beta_two = 0.999
adam_eps = 1e-06
decay_rate = 0.01
clip_fraction = 0.5
lamb_step = 10.0


def param_layout():
    return [
        ("latent", (LAT, D)),
        ("episode", (EPISODES, D)),
        ("tok_norm", (2, DIN)),
        ("lat_norms", (8, D)),
        ("w_kv", (DIN, 2 * CH)),
        ("w_q", (D, CH)),
        ("w_o", (CH, D)),
        ("w_qkv", (D, 3 * D)),
        ("w_so", (D, D)),
        ("w_up", (2, D, FF)),
        ("w_down", (2, FF, D)),
        ("hid_bias", (2, FF)),
        ("out_bias", (4, D)),
    ]


def split_flat(flat_vector):
    pieces = {}
    offset = 0
    for tensor_name, tensor_shape in param_layout():
        entries = math.prod(tensor_shape)
        pieces[tensor_name] = flat_vector[offset : offset + entries].reshape(tensor_shape)
        offset += entries
    return pieces


def layer_norm(inputs, norm_gain, norm_bias):
    row_mean = jnp.mean(inputs, axis=-1, keepdims=True)
    centered = inputs - row_mean
    row_var = jnp.mean(centered * centered, axis=-1, keepdims=True)
    return centered * lax.rsqrt(row_var + norm_eps) * norm_gain + norm_bias


def gelu_exact(inputs):
    return jax.nn.gelu(inputs, approximate=False)


def mlp_forward(row_data, norm_gain, norm_bias, w_up, up_bias, w_down, down_bias):
    normed_full, norm_pull = jax.vjp(layer_norm, row_data, norm_gain, norm_bias)
    normed = normed_full.astype(jnp.bfloat16)
    pre_act = jnp.dot(normed, w_up, preferred_element_type=jnp.float32) + up_bias
    active_full, gelu_pull = jax.vjp(gelu_exact, pre_act)
    activation = active_full.astype(jnp.bfloat16)
    branch_out = jnp.dot(activation, w_down, preferred_element_type=jnp.float32) + down_bias
    return (branch_out, (norm_pull, normed, gelu_pull, activation))


def mlp_backward(grad_after, kept, w_up, w_down):
    norm_pull, normed, gelu_pull, activation = kept
    grad_low = grad_after.astype(jnp.bfloat16)
    grad_down = jnp.einsum("rf,rd->fd", activation, grad_low, preferred_element_type=jnp.float32)
    grad_down_bias = jnp.sum(grad_low.astype(jnp.float32), axis=0)
    grad_active = jnp.einsum("rd,fd->rf", grad_low, w_down, preferred_element_type=jnp.float32)
    grad_pre = gelu_pull(grad_active)[0].astype(jnp.bfloat16)
    grad_up = jnp.einsum("rd,rf->df", normed, grad_pre, preferred_element_type=jnp.float32)
    grad_up_bias = jnp.sum(grad_pre.astype(jnp.float32), axis=0)
    grad_normed = jnp.einsum("rf,df->rd", grad_pre, w_up, preferred_element_type=jnp.float32)
    grad_rows, grad_gain, grad_bias = norm_pull(grad_normed)
    return (
        grad_after + grad_rows,
        (grad_gain, grad_bias, grad_up, grad_up_bias, grad_down, grad_down_bias),
    )


def self_forward(frame_block):
    heads_view = frame_block.reshape(LAT, 3, HEADS, HEAD_DIM)
    score_raw = jnp.einsum(
        "qhd,khd->hqk", heads_view[:, 0], heads_view[:, 1], preferred_element_type=jnp.float32
    ) * HEAD_DIM ** (-0.5)
    row_top = jnp.max(score_raw, axis=-1)
    log_total = row_top + jnp.log(jnp.sum(jnp.exp(score_raw - row_top[..., None]), axis=-1))
    attn_prob = jnp.exp(score_raw - log_total[..., None]).astype(jnp.bfloat16)
    accumulated = jnp.einsum(
        "hqk,khd->qhd", attn_prob, heads_view[:, 2], preferred_element_type=jnp.float32
    )
    return (accumulated.reshape(LAT, D), log_total)


def self_backward(inputs):
    frame_block, accumulated, log_total, grad_out = inputs
    heads_view = frame_block.reshape(LAT, 3, HEADS, HEAD_DIM)
    query_part = heads_view[:, 0]
    key_part = heads_view[:, 1]
    value_part = heads_view[:, 2]
    scale_self = HEAD_DIM ** (-0.5)
    score_raw = (
        jnp.einsum("qhd,khd->hqk", query_part, key_part, preferred_element_type=jnp.float32)
        * scale_self
    )
    prob_full = jnp.exp(score_raw - log_total[..., None])
    attn_prob = prob_full.astype(jnp.bfloat16)
    grad_heads = grad_out.reshape(LAT, HEADS, HEAD_DIM)
    row_delta = jnp.sum(
        grad_heads.astype(jnp.float32) * accumulated.reshape(LAT, HEADS, HEAD_DIM), axis=-1
    ).T
    grad_value = jnp.einsum(
        "hqk,qhd->khd", attn_prob, grad_heads, preferred_element_type=jnp.float32
    )
    grad_prob = jnp.einsum(
        "qhd,khd->hqk", grad_heads, value_part, preferred_element_type=jnp.float32
    )
    grad_score = (prob_full * (grad_prob - row_delta[..., None])).astype(jnp.bfloat16)
    grad_query = (
        jnp.einsum("hqk,khd->qhd", grad_score, key_part, preferred_element_type=jnp.float32)
        * scale_self
    )
    grad_key = (
        jnp.einsum("hqk,qhd->khd", grad_score, query_part, preferred_element_type=jnp.float32)
        * scale_self
    )
    stacked = jnp.stack([grad_query, grad_key, grad_value], axis=1)
    return stacked.reshape(LAT, 3 * D).astype(jnp.bfloat16)


def latent_forward(initial, cross_out, weights, norm_rows, out_bias, hid_bias, self_mix):
    hidden_one = (
        initial
        + jnp.dot(cross_out, weights["w_o"], preferred_element_type=jnp.float32)
        + out_bias[0]
    )
    branch_one, kept_one = mlp_forward(
        hidden_one,
        norm_rows[2],
        norm_rows[3],
        weights["w_up"][0],
        hid_bias[0],
        weights["w_down"][0],
        out_bias[1],
    )
    hidden_two = hidden_one + branch_one
    sa_full, sa_pull = jax.vjp(layer_norm, hidden_two, norm_rows[4], norm_rows[5])
    sa_in = sa_full.astype(jnp.bfloat16)
    qkv_rows = jnp.dot(sa_in, weights["w_qkv"], preferred_element_type=jnp.float32).astype(
        jnp.bfloat16
    )
    mixed, self_kept = self_mix(qkv_rows)
    hidden_three = (
        hidden_two
        + jnp.dot(mixed, weights["w_so"], preferred_element_type=jnp.float32)
        + out_bias[2]
    )
    branch_two, kept_two = mlp_forward(
        hidden_three,
        norm_rows[6],
        norm_rows[7],
        weights["w_up"][1],
        hid_bias[1],
        weights["w_down"][1],
        out_bias[3],
    )
    return (hidden_three + branch_two, (kept_one, sa_pull, sa_in, mixed, self_kept, kept_two))


def latent_backward(grad_four, state, weights, self_back):
    kept_one, sa_pull, sa_in, mixed, self_kept, kept_two = state
    grad_three, mlp_two_grads = mlp_backward(
        grad_four, kept_two, weights["w_up"][1], weights["w_down"][1]
    )
    grad_branch = grad_three.astype(jnp.bfloat16)
    grad_so = jnp.einsum("rd,re->de", mixed, grad_branch, preferred_element_type=jnp.float32)
    grad_so_bias = jnp.sum(grad_branch.astype(jnp.float32), axis=0)
    grad_mixed = jnp.einsum(
        "re,de->rd", grad_branch, weights["w_so"], preferred_element_type=jnp.float32
    ).astype(jnp.bfloat16)
    grad_qkv_rows = self_back(grad_mixed, self_kept)
    grad_qkv = jnp.einsum("rd,re->de", sa_in, grad_qkv_rows, preferred_element_type=jnp.float32)
    grad_sa_in = jnp.einsum(
        "re,de->rd", grad_qkv_rows, weights["w_qkv"], preferred_element_type=jnp.float32
    )
    grad_two_part, grad_sa_gain, grad_sa_bias = sa_pull(grad_sa_in)
    grad_two = grad_three + grad_two_part
    grad_one, mlp_one_grads = mlp_backward(
        grad_two, kept_one, weights["w_up"][0], weights["w_down"][0]
    )
    return (
        grad_one,
        (grad_so, grad_so_bias, grad_qkv, grad_sa_gain, grad_sa_bias, mlp_one_grads, mlp_two_grads),
    )


def body(tokens, frame_ids, episodes, master, moment_one, moment_two, latent_grad):
    lat_count = lax.axis_size("lat")
    lat_index = lax.axis_index("lat")
    shard_len = master.shape[0]
    whole_flat = lax.all_gather(master.astype(jnp.bfloat16), "lat", axis=0, tiled=True)
    weights = split_flat(whole_flat)
    norm_rows = weights["lat_norms"].astype(jnp.float32)
    out_bias = weights["out_bias"].astype(jnp.float32)
    hid_bias = weights["hid_bias"].astype(jnp.float32)
    tok_norm = weights["tok_norm"].astype(jnp.float32)
    token_rows = tokens[0].astype(jnp.float32)
    tok_full, token_pull = jax.vjp(layer_norm, token_rows, tok_norm[0], tok_norm[1])
    tok_normed = tok_full.astype(jnp.bfloat16)
    key_value = jnp.dot(tok_normed, weights["w_kv"], preferred_element_type=jnp.float32).astype(
        jnp.bfloat16
    )
    frame_tag = frame_ids[0].astype(jnp.bfloat16)
    all_keys, all_tags = (
        lax.all_gather(key_value, "lat", axis=0, tiled=True),
        lax.all_gather(frame_tag, "lat", axis=0, tiled=True),
    )
    total_keys = all_keys.shape[0]
    tag_values = all_tags.astype(jnp.int32)
    frame_total = episodes.shape[1]
    episode_index = jnp.arange(EPISODES, dtype=jnp.int32)
    scale_cross = CH ** (-0.5)
    row_count = LAT // lat_count
    latent_base = lax.dynamic_slice_in_dim(
        weights["latent"], lat_index * row_count, row_count, 0
    ).astype(jnp.float32)
    episode_match = episodes[0][:, None] == episode_index[None, :]
    episode_rows = jnp.dot(
        episode_match.astype(jnp.bfloat16), weights["episode"], preferred_element_type=jnp.float32
    )
    initial = (latent_base[None, :, :] + episode_rows[:, None, :]).reshape(
        frame_total * row_count, D
    )
    rows_total = initial.shape[0]
    query_full, query_pull = jax.vjp(layer_norm, initial, norm_rows[0], norm_rows[1])
    query_in = query_full.astype(jnp.bfloat16)
    queries = jnp.dot(query_in, weights["w_q"], preferred_element_type=jnp.float32).astype(
        jnp.bfloat16
    )
    block_len = min(total_keys, 2048)
    block_count = total_keys // block_len
    row_frame = jnp.arange(rows_total, dtype=jnp.int32) // row_count

    def block_scores(key_block, tag_block):
        score_raw = (
            jnp.einsum("rc,kc->rk", queries, key_block[:, :CH], preferred_element_type=jnp.float32)
            * scale_cross
        )
        visible = row_frame[:, None] == tag_block[None, :]
        return (jnp.where(visible, score_raw, masked_fill), visible)

    key_blocks = all_keys.reshape(block_count, block_len, 2 * CH)
    tag_blocks = tag_values.reshape(block_count, block_len)

    def stats_step(running, blocks):
        run_max, run_sum = running
        masked, visible = block_scores(blocks[0], blocks[1])
        new_max = jnp.maximum(run_max, jnp.max(masked, axis=1))
        block_sum = jnp.sum(jnp.where(visible, jnp.exp(masked - new_max[:, None]), 0.0), axis=1)
        return ((new_max, run_sum * jnp.exp(run_max - new_max) + block_sum), None)

    start_stats = (
        jnp.full((rows_total,), masked_fill, jnp.float32),
        jnp.zeros((rows_total,), jnp.float32),
    )
    (row_max, row_sum), unused = lax.scan(stats_step, start_stats, (key_blocks, tag_blocks))
    log_total = row_max + jnp.log(row_sum)

    def output_step(running, blocks):
        masked, visible = block_scores(blocks[0], blocks[1])
        attn_prob = jnp.where(visible, jnp.exp(masked - log_total[:, None]), 0.0).astype(
            jnp.bfloat16
        )
        return (
            running + jnp.dot(attn_prob, blocks[0][:, CH:], preferred_element_type=jnp.float32),
            None,
        )

    cross_acc, unused = lax.scan(
        output_step, jnp.zeros((rows_total, CH), jnp.float32), (key_blocks, tag_blocks)
    )

    def self_mix(qkv_rows):
        qkv_frames = lax.all_to_all(
            qkv_rows.reshape(frame_total, row_count, 3 * D),
            "lat",
            split_axis=0,
            concat_axis=1,
            tiled=True,
        )
        self_acc, self_total = lax.map(self_forward, qkv_frames)
        self_rows = lax.all_to_all(
            self_acc.astype(jnp.bfloat16), "lat", split_axis=1, concat_axis=0, tiled=True
        )
        return (self_rows.reshape(rows_total, D), (qkv_frames, self_acc, self_total))

    def self_back(grad_mixed, self_kept):
        qkv_frames, self_acc, self_total = self_kept
        grad_mixed_frames = lax.all_to_all(
            grad_mixed.reshape(frame_total, row_count, D),
            "lat",
            split_axis=0,
            concat_axis=1,
            tiled=True,
        )
        grad_qkv_frames = lax.map(
            self_backward, (qkv_frames, self_acc, self_total, grad_mixed_frames)
        )
        return lax.all_to_all(
            grad_qkv_frames, "lat", split_axis=1, concat_axis=0, tiled=True
        ).reshape(rows_total, 3 * D)

    cross_out = cross_acc.astype(jnp.bfloat16)
    hidden_four, latent_state = latent_forward(
        initial, cross_out, weights, norm_rows, out_bias, hid_bias, self_mix
    )
    latents_out = hidden_four.astype(jnp.bfloat16).reshape(1, frame_total, row_count, D)
    grad_four = latent_grad[0].reshape(rows_total, D).astype(jnp.float32)
    grad_one, latent_grads = latent_backward(grad_four, latent_state, weights, self_back)
    grad_cross_branch = grad_one.astype(jnp.bfloat16)
    grad_w_o = jnp.einsum(
        "rc,rd->cd", cross_out, grad_cross_branch, preferred_element_type=jnp.float32
    )
    grad_cross_bias = jnp.sum(grad_cross_branch.astype(jnp.float32), axis=0)
    grad_cross_out = jnp.einsum(
        "rd,cd->rc", grad_cross_branch, weights["w_o"], preferred_element_type=jnp.float32
    ).astype(jnp.bfloat16)
    cross_delta = jnp.sum(grad_cross_out.astype(jnp.float32) * cross_acc, axis=1)
    back_key_blocks = all_keys.reshape(block_count, block_len, 2 * CH)
    back_tag_blocks = tag_values.reshape(block_count, block_len)

    def key_grad_step(grad_query, blocks):
        key_block, tag_block = blocks
        masked, visible = block_scores(key_block, tag_block)
        prob_full = jnp.where(visible, jnp.exp(masked - log_total[:, None]), 0.0)
        attn_prob = prob_full.astype(jnp.bfloat16)
        grad_value = jnp.einsum(
            "rk,rc->kc", attn_prob, grad_cross_out, preferred_element_type=jnp.float32
        )
        grad_prob = jnp.einsum(
            "rc,kc->rk", grad_cross_out, key_block[:, CH:], preferred_element_type=jnp.float32
        )
        grad_score = (prob_full * (grad_prob - cross_delta[:, None])).astype(jnp.bfloat16)
        grad_query = (
            grad_query
            + jnp.einsum(
                "rk,kc->rc", grad_score, key_block[:, :CH], preferred_element_type=jnp.float32
            )
            * scale_cross
        )
        grad_key = (
            jnp.einsum("rk,rc->kc", grad_score, queries, preferred_element_type=jnp.float32)
            * scale_cross
        )
        return (grad_query, jnp.concatenate([grad_key, grad_value], axis=1))

    grad_queries, key_terms = lax.scan(
        key_grad_step, jnp.zeros((rows_total, CH), jnp.float32), (back_key_blocks, back_tag_blocks)
    )
    key_terms = key_terms.reshape(total_keys, 2 * CH)
    grad_kv = lax.psum_scatter(
        key_terms.astype(jnp.bfloat16), "lat", scatter_dimension=0, tiled=True
    )
    grad_w_kv = jnp.einsum("td,tc->dc", tok_normed, grad_kv, preferred_element_type=jnp.float32)
    grad_tok_normed = jnp.einsum(
        "tc,dc->td", grad_kv, weights["w_kv"], preferred_element_type=jnp.float32
    )
    grad_tokens, grad_tok_gain, grad_tok_bias = token_pull(grad_tok_normed)
    token_grad = grad_tokens.astype(jnp.bfloat16)[None]
    grad_query_low = grad_queries.astype(jnp.bfloat16)
    grad_w_q = jnp.einsum("rd,rc->dc", query_in, grad_query_low, preferred_element_type=jnp.float32)
    grad_query_in = jnp.einsum(
        "rc,dc->rd", grad_query_low, weights["w_q"], preferred_element_type=jnp.float32
    )
    grad_start_part, grad_q_gain, grad_q_bias = query_pull(grad_query_in)
    grad_start = (grad_one + grad_start_part).reshape(frame_total, row_count, D)
    latent_rows_grad = jnp.sum(grad_start, axis=0)
    frame_sums = jnp.sum(grad_start, axis=1)
    grad_episode = jnp.sum(
        episode_match.astype(jnp.float32)[:, :, None] * frame_sums[:, None, :], axis=0
    )
    grad_latent = lax.dynamic_update_slice(
        jnp.zeros((LAT, D), jnp.float32), latent_rows_grad, (lat_index * row_count, lat_index * 0)
    )
    grad_so, grad_so_bias, grad_qkv, grad_sa_gain, grad_sa_bias, mlp_one_grads, mlp_two_grads = (
        latent_grads
    )
    one_gain, one_bias, one_up, one_up_bias, one_down, one_down_bias = mlp_one_grads
    two_gain, two_bias, two_up, two_up_bias, two_down, two_down_bias = mlp_two_grads
    grads = {
        "latent": grad_latent,
        "episode": grad_episode,
        "tok_norm": jnp.stack([grad_tok_gain, grad_tok_bias]),
        "lat_norms": jnp.stack(
            [
                grad_q_gain,
                grad_q_bias,
                one_gain,
                one_bias,
                grad_sa_gain,
                grad_sa_bias,
                two_gain,
                two_bias,
            ]
        ),
        "w_kv": grad_w_kv,
        "w_q": grad_w_q,
        "w_o": grad_w_o,
        "w_qkv": grad_qkv,
        "w_so": grad_so,
        "w_up": jnp.stack([one_up, two_up]),
        "w_down": jnp.stack([one_down, two_down]),
        "hid_bias": jnp.stack([one_up_bias, two_up_bias]),
        "out_bias": jnp.stack([grad_cross_bias, one_down_bias, grad_so_bias, two_down_bias]),
    }
    layout = param_layout()
    local_flat = jnp.concatenate(
        [grads[tensor_name].reshape(-1) for tensor_name, tensor_shape in layout]
    )
    summed = lax.psum(local_flat.astype(jnp.bfloat16), "kf")
    grad_shard = lax.psum_scatter(summed, "lat", scatter_dimension=0, tiled=True).astype(
        jnp.float32
    )
    starts_list = []
    ends_list = []
    offset = 0
    bias_offset = 0
    for tensor_name, tensor_shape in layout:
        if tensor_name == "hid_bias":
            bias_offset = offset
        starts_list.append(offset)
        offset += math.prod(tensor_shape)
        ends_list.append(offset)
    shard_base = lat_index * shard_len
    positions = shard_base + jnp.arange(shard_len, dtype=jnp.int32)
    segment_hot = (
        (positions[None, :] >= jnp.array(starts_list, jnp.int32)[:, None])
        & (positions[None, :] < jnp.array(ends_list, jnp.int32)[:, None])
    ).astype(jnp.float32)
    bias_local = bias_offset + jnp.arange(2 * FF, dtype=jnp.int32) - shard_base
    bias_inside = (bias_local >= 0) & (bias_local < shard_len)
    bias_picked = jnp.where(bias_inside, grad_shard[jnp.clip(bias_local, 0, shard_len - 1)], 0.0)
    local_grad_sq = jnp.sum(grad_shard * grad_shard)
    local_weight_sq = jnp.sum(segment_hot * (master * master)[None, :], axis=1)
    total_sq, weight_sq, bias_total = lax.psum((local_grad_sq, local_weight_sq, bias_picked), "lat")
    bias_grad = bias_total.reshape(2, FF)
    clip_scale = jnp.minimum(1.0, clip_fraction * math.sqrt(NPARAM) / (jnp.sqrt(total_sq) + 1e-06))
    clipped = clip_scale * grad_shard
    new_one = beta_one * moment_one + (1.0 - beta_one) * clipped
    new_two = beta_two * moment_two + (1.0 - beta_two) * clipped * clipped
    first_hat = new_one / (1.0 - beta_one**lamb_step)
    second_hat = new_two / (1.0 - beta_two**lamb_step)
    lamb_update = first_hat / (jnp.sqrt(second_hat) + adam_eps) + decay_rate * master
    local_update_sq = jnp.sum(segment_hot * (lamb_update * lamb_update)[None, :], axis=1)
    update_sq = lax.psum(local_update_sq, "lat")
    trust = jnp.sqrt(weight_sq) / (jnp.sqrt(update_sq) + 1e-06)
    return (latents_out, token_grad, grad_shard, lamb_update, new_one, new_two, trust, bias_grad)


def solution(mesh):
    return jax.shard_map(
        body,
        mesh=mesh,
        in_specs=(
            P("kf", "lat", None),
            P("kf", "lat"),
            P("kf", None),
            P("lat"),
            P("lat"),
            P("lat"),
            P("kf", None, "lat", None),
        ),
        out_specs=(
            P("kf", None, "lat", None),
            P("kf", "lat", None),
            P("lat"),
            P("lat"),
            P("lat"),
            P("lat"),
            P(),
            P(),
        ),
        check_vma=False,
    )
```

profile of v0, /device:TPU:0, one launch (start us, length us, event | category | flops | bytes accessed | tf_op | source)
XLA Modules:
  0.0 1187.2 jit_solution(2054575425345923392)
XLA Ops:
  10.4 10.4 all-gather
  21.3 58.4 %all-gather.4.cloned.1.call-done = bf16[5619712]{0:T(1024)(128)(2,1)} async-done(((bf16[702464]{0:T(1024)(128)(2,1)}), bf16[5619712]{0:T(1024)(128)(2,1)}) %all-gather.4.cloned.1.call-update) | async-done | bytes 11239440 | tf_op jit(solution)/shard_map/all_gather | solution.py:215
  89.7 5.9 fusion.138
  113.0 33.2 %while.61 = (s32[]{:T(128)}, f32[2048]{0:T(1024)S(1)}, f32[2048]{0:T(1024)S(1)}, s32[2,2048]{1,0:T(2,128)S(1)}, bf16[2,2048,128]{2,1,0:T(8,128)(2,1)}, /*index=5*/bf16[2048,64]{1,0:T(8,128)(2,1)S(1)}, s32[]{:T(128)}, s32[]{:T(128)}) while((s32[]{:T(128)}, f32[2048]{0:T(1024)S(1)}, f32[2048]{0:T(1024)S(1)}, ...), condition=%wide.region_7.8_spmd.clone, body=%wide.region_4.7_spmd.clone.sunk | while | flops 578840576 | bytes 35553380 | solution.py:280
  114.2 7.1 fusion.243
  121.2 8.4 fusion.244
  130.8 7.1 fusion.243
  137.8 8.4 fusion.244
  146.3 13.5 %while.62 = (s32[]{:T(128)}, f32[2048,64]{0,1:T(8,128)S(1)}, s32[2,2048]{1,0:T(2,128)S(1)}, bf16[2,2048,128]{2,1,0:T(8,128)(2,1)}, bf16[2048,64]{1,0:T(8,128)(2,...) while((s32[]{:T(128)}, f32[2048,64]{0,1:T(8,128)S(1)}, s32[2,2048]{1,0:T(2,128)S(1)}, ...), condition=%wide.region_9.10_spmd.clone, body=%wide.region_8.9_spmd.clone.sunk | while | flops 1099186176 | bytes 3719271 | solution.py:293
  166.4 43.6 %multiply_convert_fusion.2 = (bf16[2048,2048]{1,0:T(8,128)(2,1)S(1)}, f32[2048,2048]{1,0:T(8,128)}, f32[2048,2048]{1,0:T(8,128)}) fusion(f32[2048]{0:T(1024)S(1)} %get-tuple-element.552, bf16[512,2048]{1,0:T(8,128)(2,1)S(1)} %copy-done.38, f32[2048,512]{1,0:T(8,128)S(1)} %get-tuple-element.568, f32[512]{0:T(512)S(1)} %get-tuple-element.557, ...), kind=kOutput, calls=%fused_computation.134 | convolution fusion | flops 4577034240 | bytes 48263168 | tf_op jit(solution)/shard_map/dot_general | solution.py:71
  231.1 71.6 %all-to-all-done = bf16[32,64,1536]{2,1,0:T(8,128)(2,1)} async-done(((bf16[32,64,1536]{2,1,0:T(8,128)(2,1)}), bf16[32,64,1536]{2,1,0:T(8,128)(2,1)}, u32[]{:S(2)}, u32[]{:S(2)}) %all-to-all-start) | async-done | bytes 6291488 | tf_op jit(solution)/shard_map/all_to_all | solution.py:298
  302.7 6.1 copy.75
  308.8 8.7 copy.76
  317.5 29.7 %while.59 = (s32[]{:T(128)}, f32[4,512,512]{1,2,0:T(8,128)}, f32[4,8,512]{2,1,0:T(8,128)}, bf16[4,512,1536]{1,2,0:T(8,128)(2,1)}, s32[]{:T(128)}) while((s32[]{:T(128)}, f32[4,512,512]{1,2,0:T(8,128)}, f32[4,8,512]{2,1,0:T(8,128)}, bf16[4,512,1536]{1,2,0:T(8,128)(2,1)}, s32[]{:T(128)}) %tuple.184), condition=%wide.region_17.18_spmd, body=%wide.region_14.17_spmd.sunk | while | flops 553644032 | bytes 33162304 | solution.py:305
  364.9 17.5 %all-to-all-done.1 = bf16[4,512,512]{2,0,1:T(4,128)(2,1)S(1)} async-done(((bf16[4,512,512]{2,0,1:T(4,128)(2,1)}), bf16[4,512,512]{2,0,1:T(4,128)(2,1)S(1)}, u32[]{:S(2)}, u32[]{:S(2)}) %all-to-all-start.1) | async-done | bytes 2097184 | tf_op jit(solution)/shard_map/all_to_all | solution.py:306
  390.0 43.7 %multiply_convert_fusion.1 = (bf16[2048,2048]{1,0:T(8,128)(2,1)}, f32[2048,2048]{1,0:T(8,128)}, f32[2048,2048]{1,0:T(8,128)}) fusion(f32[2048]{0:T(1024)S(1)} %copy-done.100, bf16[512,2048]{1,0:T(8,128)(2,1)S(1)} %copy-done.41, f32[2048,512]{1,0:T(8,128)S(1)} %get-tuple-element.573, f32[512]{0:T(512)S(1)} %copy-done.117, f32[512]{0:T(512)S(1)} %copy-done.106, ...), kind=kOutput, calls=%fused_computation.121 | convolution fusion | flops 4577034240 | bytes 48263168 | tf_op jit(solution)/shard_map/dot_general | solution.py:71
  433.7 19.5 %fusion.148 = (bf16[2048]{0:T(1024)(128)(2,1)S(1)}, bf16[2048,2048]{1,0:T(8,128)(2,1)}) fusion(f32[2048,2048]{1,0:T(8,128)} %get-tuple-element.531, bf16[2048,512]{1,0:T(8,128)(2,1)S(1)} %bitcast.358, bf16[2048,512]{1,0:T(8,128)(2,1)} %slice.328, f32[2048,2048]{1,0:T(8,128)} %get-tuple-element.574, f32[2048]{0:T(1024)S(1)} %copy-done.100), kind=kOutput, calls=%fused_computation.321 | convolution fusion | flops 4362074112 | bytes 46149632 | tf_op jit(solution)/shard_map/rd,fd->rf/dot_general | solution.py:83
  453.3 11.4 multiply_reduce_fusion.2
  475.9 26.6 %all-to-all-done.2 = bf16[32,64,512]{2,1,0:T(8,128)(2,1)} async-done(((bf16[32,64,512]{2,1,0:T(8,128)(2,1)}), bf16[32,64,512]{2,1,0:T(8,128)(2,1)}, u32[]{:S(2)}, u32[]{:S(2)}) %all-to-all-start.2) | async-done | bytes 2097184 | tf_op jit(solution)/shard_map/all_to_all | solution.py:313
  505.6 59.0 %while.60 = (s32[]{:T(128)}, bf16[4,512,1536]{1,2,0:T(8,128)(2,1)}, bf16[4,512,1536]{1,2,0:T(8,128)(2,1)}, f32[4,8,512]{2,1,0:T(8,128)}, bf16[4,512,512]{2,1,0:T(8,128)(2,1)}, /*index=5*/f32[4,512,512]{1,2,0:T(8,128)}, s32[]{:T(128)}) while((s32[]{:T(128)}, bf16[4,512,1536]{1,2,0:T(8,128)(2,1)}, bf16[4,512,1536]{1,2,0:T(8,128)(2,1)}, ...), condition=%wide.region_24.25_spmd, body=%wide.region_22.24_spmd.sunk | while | flops 1362620416 | bytes 58294876 | solution.py:320
  564.6 11.5 copy.83
  590.4 9.8 fusion.82
  600.2 6.3 fusion.80
  606.5 46.1 %all-to-all-done.3 = bf16[4,512,1536]{2,0,1:T(4,128)(2,1)} async-done(((bf16[4,512,1536]{2,0,1:T(4,128)(2,1)}), bf16[4,512,1536]{2,0,1:T(4,128)(2,1)}, u32[]{:S(2)}, u32[]{:S(2)}) %all-to-all-start.3) | async-done | bytes 6291488 | tf_op jit(solution)/shard_map/all_to_all | solution.py:323
  660.2 6.7 multiply_reduce_fusion.3
  672.1 6.6 fusion.81
  678.7 23.3 %fusion.149 = (bf16[2048]{0:T(1024)(128)(2,1)}, bf16[2048,2048]{1,0:T(8,128)(2,1)}) fusion(f32[2048,2048]{1,0:T(8,128)} %get-tuple-element.533, bf16[2048,512]{1,0:T(8,128)(2,1)} %slice.314, f32[2048,512]{1,0:T(8,128)} %copy-done.5, f32[2048,2048]{1,0:T(8,128)} %get-tuple-element.569, f32[2048]{0:T(1024)S(1)} %copy-done.99), kind=kOutput, calls=%fused_computation.322 | convolution fusion | flops 4363122688 | bytes 48246784 | tf_op jit(solution)/shard_map/rd,fd->rf/dot_general | solution.py:83
  702.1 11.3 multiply_reduce_fusion.4
  713.4 8.4 fusion.79
  737.8 71.3 %while.63 = (s32[]{:T(128)}, f32[2048,64]{0,1:T(8,128)}, bf16[2,2048,128]{2,1,0:T(8,128)(2,1)}, s32[2,2048]{1,0:T(2,128)S(1)}, bf16[2,2048,128]{2,1,0:T(8,128)(2...) while((s32[]{:T(128)}, f32[2048,64]{0,1:T(8,128)}, ...), condition=%wide.region_31.32_spmd.clone, body=%wide.region_30.31_spmd.clone.sunk | while | flops 2744795136 | bytes 119620312 | solution.py:371
  737.9 8.1 fusion.259
  746.0 9.3 fusion.260
  758.6 7.9 fusion.262
  767.6 5.9 fusion.261
  773.5 8.1 fusion.259
  781.6 9.3 fusion.260
  794.2 7.9 fusion.262
  803.2 5.9 fusion.261
  809.2 6.0 multiply_reduce_fusion.5
  827.7 9.0 convolution_convert_fusion.5
  868.4 156.1 %all-reduce.7.cloned.1.call-done = bf16[5619712]{0:T(1024)(128)(2,1)} async-done(((bf16[5619712]{0:T(1024)(128)(2,1)}), bf16[5619712]{0:T(1024)(128)(2,1)}) %all-reduce.7.cloned.1.call-update) | async-done | bytes 11239440
  1027.1 10.1 add_convert_fusion.2
  1038.4 52.2 %all-reduce.5.cloned.1.call-done = bf16[702464]{0:T(1024)(128)(2,1)} async-done(((bf16[702464]{0:T(1024)(128)(2,1)}), bf16[702464]{0:T(1024)(128)(2,1)}) %all-reduce.5.cloned.1.call-update) | async-done | bytes 1404944 | tf_op jit(solution)/shard_map/psum | solution.py:434
  1093.2 14.0 %psum.36 = f32[]{:T(128)} all-reduce(f32[]{:T(128)} %get-tuple-element.510), channel_id=1, replica_groups=mesh['kf'=4,'lat'=8] {'lat'}, use_global_device_ids=true, to_apply=%region_59.60 | all-reduce | flops 1 | bytes 8 | tf_op jit(solution)/shard_map/psum | solution.py:459
  1107.9 23.0 %gather_fusion = f32[4096]{0:T(1024)S(1)} fusion(f32[702464]{0:T(1024)S(1)} %get-tuple-element.511, s32[4096]{0:T(1024)S(1)} %copy-done.77), kind=kCustom, calls=%fused_computation | custom fusion | bytes 49152 | tf_op jit(solution)/shard_map/gather | solution.py:456
  1131.1 6.4 fusion.125
  1137.4 19.3 %select_reduce_fusion.1 = (f32[13]{0:T(128)S(1)}, f32[13]{0:T(128)S(1)}) fusion(f32[702464]{0:T(1024)S(1)} %get-tuple-element.548, s32[702464]{0:T(1024)S(1)} %copy-done.28, s32[13]{0:T(128)S(1)} %copy-done.129, s32[13]{0:T(128)S(1)} %copy-done.128, f32[702464]{0:T(1024)S(1)} %get-tuple-element.506), kind=kLoop, calls=%fused_computation.113 | loop fusion | flops 63924200 | bytes 8429776 | tf_op jit(solution)/shard_map/reduce_sum | solution.py:458
  1156.8 22.9 %all-reduce.1 = (f32[13]{0:T(128)S(1)}, f32[13]{0:T(128)S(1)}, f32[2,2048]{1,0:T(2,128)}) all-reduce(f32[13]{0:T(128)S(1)} %get-tuple-element.435, f32[13]{0:T(128)S(1)} %get-tuple-element.434, f32[2,2048]{1,0:T(2,128)S(1)} %reshape.624), channel_id=1, replica_groups=mesh['kf'=4,'lat'=8] {'lat'}, use_global_device_ids=true, to_apply=%region_63.64 | all-reduce | flops 4122 | bytes 32976 | tf_op jit(solution)/shard_map/psum | solution.py:469
  (566 shorter events, 303.1 us)
Async XLA Ops:
  7.2 75.7 %copy-start.111 = (s32[1,32]{1,0:T(1,128)S(1)}, s32[1,32]{1,0:T(1,128)}, u32[]{:S(2)}) copy-start(s32[1,32]{1,0:T(1,128)} %param.21) | copy-start | bytes 388
  7.2 72.5 %all-gather.4.cloned.1.call-start = ((), (), s32[]{:S(2)}) async-start(), calls=%async_computation.5 | async-start | bytes 12644352 | tf_op jit(solution)/shard_map/all_gather | solution.py:215
  10.3 102.7 %all-gather.6.cloned.1.call-start = ((), (), s32[]{:S(2)}) async-start(), calls=%async_computation.6 | async-start | bytes 1179648 | tf_op jit(solution)/shard_map/all_gather | solution.py:229
  21.0 65.9 %copy-start.87 = (f32[512]{0:T(512)}, f32[512]{0:T(512)S(1)}, u32[]{:S(2)}) copy-start(f32[512]{0:T(512)S(1)} %broadcast_multiply_fusion.4) | copy-start | bytes 6148
  21.3 60.5 %copy-start.89 = (f32[512]{0:T(512)}, f32[512]{0:T(512)S(1)}, u32[]{:S(2)}) copy-start(f32[512]{0:T(512)S(1)} %fusion.99) | copy-start | bytes 6148
  21.3 67.5 %copy-start.92 = (f32[512]{0:T(512)}, f32[512]{0:T(512)S(1)}, u32[]{:S(2)}) copy-start(f32[512]{0:T(512)S(1)} %fusion.118) | copy-start | bytes 6148
  97.2 67.5 %copy-start.104 = (f32[512]{0:T(512)}, f32[512]{0:T(512)S(1)}, u32[]{:S(2)}) copy-start(f32[512]{0:T(512)S(1)} %get-tuple-element.558) | copy-start | bytes 6148
  97.2 67.5 %copy-start.115 = (f32[512]{0:T(512)}, f32[512]{0:T(512)S(1)}, u32[]{:S(2)}) copy-start(f32[512]{0:T(512)S(1)} %get-tuple-element.557) | copy-start | bytes 6148
  102.3 57.5 %copy-start.54 = (bf16[64,512]{1,0:T(8,128)(2,1)}, bf16[64,512]{1,0:T(8,128)(2,1)S(1)}, u32[]{:S(2)}) copy-start(bf16[64,512]{1,0:T(8,128)(2,1)S(1)} %slice.304) | copy-start | bytes 196612
  163.3 46.8 %copy-start.12 = (f32[2048,512]{1,0:T(8,128)}, f32[2048,512]{1,0:T(8,128)S(1)}, u32[]{:S(2)}) copy-start(f32[2048,512]{1,0:T(8,128)S(1)} %get-tuple-element.568) | copy-start | bytes 12582916
  163.3 46.7 %copy-start.75 = (f32[2048]{0:T(1024)}, f32[2048]{0:T(1024)S(1)}, u32[]{:S(2)}) copy-start(f32[2048]{0:T(1024)S(1)} %broadcast_multiply_fusion.3) | copy-start | bytes 24580
  164.2 45.8 %copy-start.68 = (f32[2048]{0:T(1024)}, f32[2048]{0:T(1024)S(1)}, u32[]{:S(2)}) copy-start(f32[2048]{0:T(1024)S(1)} %multiply_reduce_fusion.12) | copy-start | bytes 24580
  164.8 45.3 %copy-start.83 = (f32[2048]{0:T(1024)}, f32[2048]{0:T(1024)S(1)}, u32[]{:S(2)}) copy-start(f32[2048]{0:T(1024)S(1)} %get-tuple-element.586) | copy-start | bytes 24580
  164.8 45.3 %copy-start.98 = (f32[2048]{0:T(1024)}, f32[2048]{0:T(1024)S(1)}, u32[]{:S(2)}) copy-start(f32[2048]{0:T(1024)S(1)} %get-tuple-element.552) | copy-start | bytes 24580
  166.4 46.9 %copy-start.40 = (bf16[2048,512]{1,0:T(8,128)(2,1)S(1)}, bf16[2048,512]{1,0:T(8,128)(2,1)}, u32[]{:S(2)}) copy-start(bf16[2048,512]{1,0:T(8,128)(2,1)} %slice.314) | copy-start | bytes 6291460
  166.4 46.9 %copy-start.121 = (f32[512]{0:T(512)S(1)}, f32[512]{0:T(512)}, u32[]{:S(2)}) copy-start(f32[512]{0:T(512)} %get-tuple-element.563) | copy-start | bytes 6148
  226.1 76.6 %all-to-all-start = ((bf16[32,64,1536]{2,1,0:T(8,128)(2,1)}), bf16[32,64,1536]{2,1,0:T(8,128)(2,1)}, u32[]{:S(2)}, u32[]{:S(2)}) async-start(bf16[32,64,1536]{2,1,0:T(8,128)(2,1)} %bitcast.371), calls=%async_computation | async-start | bytes 12582912 | tf_op jit(solution)/shard_map/all_to_all | solution.py:298
  352.3 30.2 %all-to-all-start.1 = ((bf16[4,512,512]{2,0,1:T(4,128)(2,1)}), bf16[4,512,512]{2,0,1:T(4,128)(2,1)S(1)}, u32[]{:S(2)}, u32[]{:S(2)}) async-start(bf16[4,512,512]{2,0,1:T(4,128)(2,1)} %copy.77), calls=%async_computation.1 | async-start | bytes 4194304 | tf_op jit(solution)/shard_map/all_to_all | solution.py:306
  356.2 26.8 %copy-start.47 = (bf16[512,512]{1,0:T(8,128)(2,1)}, bf16[512,512]{1,0:T(8,128)(2,1)S(1)}, u32[]{:S(2)}) copy-start(bf16[512,512]{1,0:T(8,128)(2,1)S(1)} %slice.320) | copy-start | bytes 1572868
  364.9 18.1 %copy-start.107 = (f32[512]{0:T(512)S(1)}, f32[512]{0:T(512)}, u32[]{:S(2)}) copy-start(f32[512]{0:T(512)} %get-tuple-element.562) | copy-start | bytes 6148
  386.8 46.9 %copy-start.14 = (f32[2048,512]{1,0:T(8,128)}, f32[2048,512]{1,0:T(8,128)S(1)}, u32[]{:S(2)}) copy-start(f32[2048,512]{1,0:T(8,128)S(1)} %get-tuple-element.573) | copy-start | bytes 12582916
  387.7 45.9 %copy-start.66 = (f32[2048]{0:T(1024)}, f32[2048]{0:T(1024)S(1)}, u32[]{:S(2)}) copy-start(f32[2048]{0:T(1024)S(1)} %multiply_reduce_fusion.10) | copy-start | bytes 24580
  389.9 43.7 %copy-start.21 = (bf16[1,32,64,512]{3,2,1,0:T(8,128)(2,1)S(1)}, bf16[1,32,64,512]{3,2,1,0:T(8,128)(2,1)}, u32[]{:S(2)}) copy-start(bf16[1,32,64,512]{3,2,1,0:T(8,128)(2,1)} %param.25) | copy-start | bytes 6291460
  471.1 31.4 %all-to-all-start.2 = ((bf16[32,64,512]{2,1,0:T(8,128)(2,1)}), bf16[32,64,512]{2,1,0:T(8,128)(2,1)}, u32[]{:S(2)}, u32[]{:S(2)}) async-start(bf16[32,64,512]{2,1,0:T(8,128)(2,1)} %bitcast.372), calls=%async_computation.2 | async-start | bytes 4194304 | tf_op jit(solution)/shard_map/all_to_all | solution.py:313
  576.1 76.5 %all-to-all-start.3 = ((bf16[4,512,1536]{2,0,1:T(4,128)(2,1)}), bf16[4,512,1536]{2,0,1:T(4,128)(2,1)}, u32[]{:S(2)}, u32[]{:S(2)}) async-start(bf16[4,512,1536]{2,0,1:T(4,128)(2,1)} %copy.83), calls=%async_computation.3 | async-start | bytes 12582912 | tf_op jit(solution)/shard_map/all_to_all | solution.py:323
  581.0 269.5 %reduce-scatter.2.cloned.1.call-start = ((), (), s32[]{:S(2)}) async-start(), calls=%async_computation.7 | async-start | bytes 1179648 | tf_op jit(solution)/shard_map/reduce_scatter | solution.py:375
  585.1 15.0 %slice-start.1 = ((s8[8388608]{0:T(1024)(128)(4,1)}), s8[4194304]{0:T(1024)(128)(4,1)S(1)}, s32[]{:S(2)}) async-start(s8[8388608]{0:T(1024)(128)(4,1)} %bitcast.393), calls=%async_computation.11 | async-start | bytes 8388608
  678.7 23.4 %copy-start.39 = (bf16[512,2048]{1,0:T(8,128)(2,1)S(1)}, bf16[512,2048]{1,0:T(8,128)(2,1)}, u32[]{:S(2)}) copy-start(bf16[512,2048]{1,0:T(8,128)(2,1)} %slice.310) | copy-start | bytes 6291460
  678.7 23.4 %copy-start.76 = (f32[2048]{0:T(1024)S(1)}, f32[2048]{0:T(1024)}, u32[]{:S(2)}) copy-start(f32[2048]{0:T(1024)} %copy-done.75) | copy-start | bytes 24580
  678.7 23.4 %copy-start.84 = (f32[2048]{0:T(1024)S(1)}, f32[2048]{0:T(1024)}, u32[]{:S(2)}) copy-start(f32[2048]{0:T(1024)} %copy-done.83) | copy-start | bytes 24580
  678.7 23.4 %copy-start.105 = (f32[512]{0:T(512)S(1)}, f32[512]{0:T(512)}, u32[]{:S(2)}) copy-start(f32[512]{0:T(512)} %copy-done.104) | copy-start | bytes 6148
  737.8 71.4 %copy-start.53 = (bf16[512,64]{1,0:T(8,128)(2,1)S(1)}, bf16[512,64]{1,0:T(8,128)(2,1)}, u32[]{:S(2)}) copy-start(bf16[512,64]{1,0:T(8,128)(2,1)} %copy-done.52) | copy-start | bytes 196612
  737.8 71.3 %copy-start.59 = (f32[2048]{0:T(1024)S(1)}, f32[2048]{0:T(1024)}, u32[]{:S(2)}) copy-start(f32[2048]{0:T(1024)} %copy-done.58) | copy-start | bytes 24580
  737.8 71.3 %copy-start.61 = (f32[2048]{0:T(1024)S(1)}, f32[2048]{0:T(1024)}, u32[]{:S(2)}) copy-start(f32[2048]{0:T(1024)} %copy-done.60) | copy-start | bytes 24580
  737.8 71.3 %copy-start.86 = (f32[512]{0:T(512)S(1)}, f32[512]{0:T(512)}, u32[]{:S(2)}) copy-start(f32[512]{0:T(512)} %copy-done.85) | copy-start | bytes 6148
  737.8 20.1 %copy-start.56 = (bf16[2048,64]{1,0:T(8,128)(2,1)}, bf16[2048,64]{1,0:T(8,128)(2,1)S(1)}, u32[]{:S(2)}) copy-start(bf16[2048,64]{1,0:T(8,128)(2,1)S(1)} %get-tuple-element.903) | copy-start | bytes 786436 | tf_op jit(solution)/shard_map/while
  773.5 20.1 %copy-start.56 = (bf16[2048,64]{1,0:T(8,128)(2,1)}, bf16[2048,64]{1,0:T(8,128)(2,1)S(1)}, u32[]{:S(2)}) copy-start(bf16[2048,64]{1,0:T(8,128)(2,1)S(1)} %get-tuple-element.903) | copy-start | bytes 786436 | tf_op jit(solution)/shard_map/while
  815.2 209.3 %all-reduce.7.cloned.1.call-start = ((), (), s32[]{:S(2)}) async-start(), calls=%async_computation.9 | async-start | bytes 22478848
  827.7 13.8 %copy-start.20 = (f32[2048,64]{0,1:T(8,128)S(1)}, f32[2048,64]{0,1:T(8,128)}, u32[]{:S(2)}) copy-start(f32[2048,64]{0,1:T(8,128)} %get-tuple-element.198) | copy-start | bytes 1572868
  827.7 13.8 %copy-start.23 = (bf16[2048,512]{1,0:T(8,128)(2,1)S(1)}, bf16[2048,512]{1,0:T(8,128)(2,1)}, u32[]{:S(2)}) copy-start(bf16[2048,512]{1,0:T(8,128)(2,1)} %copy-done.22) | copy-start | bytes 6291460
  836.7 13.7 %copy-start.36 = (bf16[1,512,256]{2,1,0:T(8,128)(2,1)S(1)}, bf16[1,512,256]{2,1,0:T(8,128)(2,1)}, u32[]{:S(2)}) copy-start(bf16[1,512,256]{2,1,0:T(8,128)(2,1)} %param.19) | copy-start | bytes 786436
  842.0 15.4 %copy-start.31 = (bf16[786432]{0:T(1024)(128)(2,1)S(1)}, bf16[786432]{0:T(1024)(128)(2,1)}, u32[]{:S(2)}) copy-start(bf16[786432]{0:T(1024)(128)(2,1)} %reshape.618) | copy-start | bytes 4718596
  842.3 16.4 %copy-start.42 = (bf16[64,4,8,128]{3,1,2,0:T(4,128)(2,1)S(1)}, bf16[64,4,8,128]{3,1,2,0:T(4,128)(2,1)}, u32[]{:S(2)}) copy-start(bf16[64,4,8,128]{3,1,2,0:T(4,128)(2,1)} %copy.135) | copy-start | bytes 1572868
  866.6 160.5 %copy-start.37 = (bf16[2048,512]{1,0:T(8,128)(2,1)S(1)}, bf16[2048,512]{1,0:T(8,128)(2,1)}, u32[]{:S(2)}) copy-start(bf16[2048,512]{1,0:T(8,128)(2,1)} %slice.328) | copy-start | bytes 6291460
  866.6 160.5 %copy-start.120 = (f32[512]{0:T(512)S(1)}, f32[512]{0:T(512)}, u32[]{:S(2)}) copy-start(f32[512]{0:T(512)} %get-tuple-element.561) | copy-start | bytes 6148
  866.6 223.9 %all-reduce.5.cloned.1.call-start = ((), (), s32[]{:S(2)}) async-start(), calls=%async_computation.8 | async-start | bytes 2809856 | tf_op jit(solution)/shard_map/psum | solution.py:434
  1037.1 70.8 %copy-start.77 = (s32[4096]{0:T(1024)S(1)}, s32[4096]{0:T(1024)}, u32[]{:S(2)}) copy-start(s32[4096]{0:T(1024)} %broadcast_clamp_fusion) | copy-start | bytes 49156
  1093.2 37.8 %copy-start.1 = (f32[702464]{0:T(1024)}, f32[702464]{0:T(1024)S(1)}, u32[]{:S(2)}) copy-start(f32[702464]{0:T(1024)S(1)} %get-tuple-element.511) | copy-start | bytes 8429572
  (101 other events, 601.7 us)
Sparse Core Ops, SparseCore 0:
  10.5 69.1 all-gather.3
  88.9 23.4 all-gather.5
  815.3 35.1 reduce-scatter.1
  866.7 157.7 all-reduce.6
  1027.4 63.0 all-reduce.4
where the time goes:
time: 1190 us
  waiting for transfers between devices  433 us (36%)
  matrix products  383 us (32%)
  local copies, waits for them, and re-layouts  193 us (16%)
  other arithmetic  93.4 us (8%)
  blocking collectives  47.3 us (4%)
  starting transfers between devices  18.4 us (2%)
  between operations  17.6 us (1%)
    unnamed x6, waiting for transfers between devices  156 us
    dot_general x2, matrix products, mlp_forward(): jnp.dot(normed, w_up, preferred_element_type=jnp.float32) + up_bias  87.3 us
    all_to_all x1, waiting for transfers between devices, self_mix(): lax.all_to_all(qkv_rows.reshape(frame_total, row_count, 3 * D), 'lat', sp...  71.6 us
    all_gather x1, waiting for transfers between devices, body(): lax.all_gather(master.astype(jnp.bfloat16), 'lat', axis=0, tiled=True)  58.4 us
    psum x1, waiting for transfers between devices, body(): summed = lax.psum(local_flat.astype(jnp.bfloat16), 'kf')  52.2 us
    unnamed x290, local copies, waits for them, and re-layouts  50.8 us
    all_to_all x1, waiting for transfers between devices, self_back(): lax.all_to_all(grad_qkv_frames, 'lat', split_axis=1, concat_axis=0, tiled...  46.1 us
    dot_general x2, matrix products, mlp_backward(): jnp.einsum('rd,fd->rf', grad_low, w_down, preferred_element_type=jnp.floa...  42.9 us
  transfers between devices with their start and end apart: 9, of which 8 were waited for; matrix products, arithmetic and copies ran while one was open for 8% of the time, Pallas kernels for 0%

commit v1 on v0

v1 whole, which is shorter than its diff:
```python
import functools
import math

import jax
import jax.numpy as jnp
from jax import lax
from jax.experimental import pallas as pl
from jax.experimental.pallas import tpu as pltpu
from jax.sharding import PartitionSpec as P

DIN = 256
D = 512
LAT = 512
CH = 64
HEADS = 8
HEAD_DIM = 64
FF = 2048
EPISODES = 11
NPARAM = 5619712
LANES = 128

norm_eps = 1e-05
masked_fill = -1e30
beta_one = 0.9
beta_two = 0.999
adam_eps = 1e-06
decay_rate = 0.01
clip_fraction = 0.5
lamb_step = 10.0

BF = jnp.bfloat16
F32 = jnp.float32
MIB = 1024 * 1024


def param_layout():
    return [
        ("latent", (LAT, D)),
        ("episode", (EPISODES, D)),
        ("tok_norm", (2, DIN)),
        ("lat_norms", (8, D)),
        ("w_kv", (DIN, 2 * CH)),
        ("w_q", (D, CH)),
        ("w_o", (CH, D)),
        ("w_qkv", (D, 3 * D)),
        ("w_so", (D, D)),
        ("w_up", (2, D, FF)),
        ("w_down", (2, FF, D)),
        ("hid_bias", (2, FF)),
        ("out_bias", (4, D)),
    ]


def split_flat(flat_vector):
    pieces = {}
    offset = 0
    for tensor_name, tensor_shape in param_layout():
        entries = math.prod(tensor_shape)
        pieces[tensor_name] = flat_vector[offset : offset + entries].reshape(tensor_shape)
        offset += entries
    return pieces


def layer_norm(inputs, norm_gain, norm_bias):
    row_mean = jnp.mean(inputs, axis=-1, keepdims=True)
    centered = inputs - row_mean
    row_var = jnp.mean(centered * centered, axis=-1, keepdims=True)
    return centered * lax.rsqrt(row_var + norm_eps) * norm_gain + norm_bias


def mm(left, right):
    return jnp.dot(left, right, preferred_element_type=F32)


def mm_t(left, right):
    return lax.dot_general(left, right, (((1,), (1,)), ((), ())), preferred_element_type=F32)


def t_mm(left, right):
    return lax.dot_general(left, right, (((0,), (0,)), ((), ())), preferred_element_type=F32)


def norm_stats(rows):
    mean = jnp.mean(rows, axis=-1, keepdims=True)
    centered = rows - mean
    var = jnp.mean(centered * centered, axis=-1, keepdims=True)
    rstd = lax.rsqrt(var + norm_eps)
    return centered * rstd, rstd


def norm_back(grad, xhat, rstd, gain):
    dxh = grad * gain
    first = jnp.mean(dxh, axis=-1, keepdims=True)
    second = jnp.mean(dxh * xhat, axis=-1, keepdims=True)
    return rstd * (dxh - first - xhat * second)


def col_sum(values):
    return jnp.sum(values, axis=0, keepdims=True)


def gelu_pair(x):
    size = jnp.abs(x)
    t = pl.reciprocal(1.0 + (0.3275911 / math.sqrt(2.0)) * size, approx=True)
    e = jnp.exp(x * x * -0.5)
    poly = 0.5 * 1.061405429
    for coef in (-1.453152027, 1.421413741, -0.284496736, 0.254829592):
        poly = poly * t + 0.5 * coef
    tail = poly * t * e
    cdf = jnp.where(x >= 0.0, 1.0 - tail, tail)
    return x * cdf, cdf + x * (e * (1.0 / math.sqrt(2.0 * math.pi)))


def accumulate(first, ref, value):
    @pl.when(first)
    def _():
        ref[...] = value

    @pl.when(jnp.logical_not(first))
    def _():
        ref[...] += value


def lane_half(shape, half):
    lane = lax.broadcasted_iota(jnp.int32, shape, 1)
    return (lane >= half * 64) & (lane < half * 64 + 64)


def keep_half(values, half):
    return jnp.where(lane_half(values.shape, half), values, jnp.zeros_like(values))


def select_tokens(rank_rows, cap):
    slot = lax.broadcasted_iota(jnp.int32, (cap, LANES), 0)
    parts = []
    for r in range(rank_rows.shape[0]):
        hit = slot == rank_rows[r : r + 1, :]
        parts.append(jnp.where(hit, 1.0, 0.0).astype(BF))
    return jnp.concatenate(parts, axis=1)


def cross_scores(kvf, queries_scaled, count):
    scores = mm_t(kvf, queries_scaled)
    slot = lax.broadcasted_iota(jnp.int32, scores.shape, 0)
    return jnp.where(slot < count, scores, masked_fill)


def cross_fwd_kernel(latent, episode, norms, w_q, w_o, out_bias, kv, rank, count, h1, kvf_out, co_out, lse_out):
    cap = kvf_out.shape[1]
    start = latent[...].astype(F32) + episode[0]
    xhat, unused = norm_stats(start)
    query_in = (xhat * norms[0:1, :] + norms[1:2, :]).astype(BF)
    queries = mm(query_in, w_q[...]).astype(BF) * jnp.asarray(0.125, BF)
    chunk = 8 * LANES
    chunks = kv.shape[0] // chunk

    def step(j, acc):
        sel = select_tokens(rank[0, pl.ds(pl.multiple_of(j * 8, 8), 8), :], cap)
        return acc + mm(sel, kv[pl.ds(pl.multiple_of(j * chunk, chunk), chunk), :])

    kvf = lax.fori_loop(0, chunks, step, jnp.zeros((cap, LANES), F32)).astype(BF)
    scores = cross_scores(kvf, queries, count[0, 0:1, 0:1])
    top = jnp.max(scores, axis=0, keepdims=True)
    terms = jnp.exp(scores - top)
    total = jnp.sum(terms, axis=0, keepdims=True)
    prob = (terms * (1.0 / total)).astype(BF)
    co = t_mm(kvf, prob).T.astype(BF)
    h1[...] = start + mm(co, w_o[...]) + out_bias[0:1, :]
    kvf_out[0] = kvf
    co_out[...] = co
    lse_out[0] = top + jnp.log(total)


def cross_bwd_kernel(
    latent, episode, norms, w_q, w_o, kvf_in, co_in, lse, rank, count, g1,
    dlatent, frame_sum, dnorm, dw_q, dw_o, dbias, dkv_t,
):
    first = pl.program_id(0) == 0
    cap = kvf_in.shape[1]
    start = latent[...].astype(F32) + episode[0]
    xhat, rstd = norm_stats(start)
    query_in = (xhat * norms[0:1, :] + norms[1:2, :]).astype(BF)
    queries = mm(query_in, w_q[...]).astype(BF) * jnp.asarray(0.125, BF)
    kvf = kvf_in[0]
    grad_one = g1[...]
    branch = grad_one.astype(BF)
    grad_co = mm_t(branch, w_o[...]).astype(BF)
    accumulate(first, dw_o, t_mm(co_in[...], branch))
    accumulate(first, dbias, col_sum(branch.astype(F32)))
    scores = cross_scores(kvf, queries, count[0, 0:1, 0:1])
    prob = jnp.exp(scores - lse[0])
    prob_low = prob.astype(BF)
    weighted = prob * mm_t(kvf, grad_co)
    grad_score = (weighted - prob * col_sum(weighted)).astype(BF)
    grad_kv = (mm(grad_score, queries) + mm(prob_low, grad_co)).astype(BF)
    grad_query = (t_mm(kvf, grad_score).T * 0.125).astype(BF)
    accumulate(first, dw_q, t_mm(query_in, grad_query))
    grad_in = mm_t(grad_query, w_q[...])
    grad_start = grad_one + norm_back(grad_in, xhat, rstd, norms[0:1, :])
    accumulate(first, dnorm, jnp.concatenate([col_sum(grad_in * xhat), col_sum(grad_in)], axis=0))
    accumulate(first, dlatent, grad_start)
    frame_sum[0] = col_sum(grad_start)
    grad_kv_t = grad_kv.T
    chunk = 8 * LANES

    @pl.when(first)
    def _():
        dkv_t[...] = jnp.zeros_like(dkv_t)

    def step(j, carry):
        sel = select_tokens(rank[0, pl.ds(pl.multiple_of(j * 8, 8), 8), :], cap)
        dkv_t[:, pl.ds(pl.multiple_of(j * chunk, chunk), chunk)] += mm(grad_kv_t, sel)
        return carry

    lax.fori_loop(0, dkv_t.shape[1] // chunk, step, 0)


FCHUNK = 512


def mlp_one_fwd_kernel(
    h1, norms, hid_bias, out_bias, w_up, w_down, w_qkv, h2, normed_out, act_out, slope_out, sa_out, qkv_out
):
    rows = h1[...]
    xhat, unused = norm_stats(rows)
    normed = (xhat * norms[2:3, :] + norms[3:4, :]).astype(BF)
    normed_out[...] = normed
    total = rows + out_bias[1:2, :]
    for c in range(FF // FCHUNK):
        at = slice(c * FCHUNK, (c + 1) * FCHUNK)
        act, slope = gelu_pair(mm(normed, w_up[:, at]) + hid_bias[0:1, at])
        act = act.astype(BF)
        act_out[:, at] = act
        slope_out[:, at] = slope.astype(BF)
        total = total + mm(act, w_down[at, :])
    h2[...] = total
    xhat, unused = norm_stats(total)
    sa_in = (xhat * norms[4:5, :] + norms[5:6, :]).astype(BF)
    sa_out[...] = sa_in
    for c in range(3):
        at = slice(c * D, (c + 1) * D)
        qkv_out[:, at] = mm(sa_in, w_qkv[:, at]).astype(BF)


def mlp_two_kernel(
    h3, grad, norms, hid_bias, out_bias, w_up, w_down,
    latents, g3, normed_out, act_out, dpre_out, dnorm, dhid, dout, slope_keep,
):
    first = pl.program_id(0) == 0
    rows = h3[...]
    xhat, rstd = norm_stats(rows)
    normed = (xhat * norms[6:7, :] + norms[7:8, :]).astype(BF)
    normed_out[...] = normed
    total = rows + out_bias[3:4, :]
    for c in range(FF // FCHUNK):
        at = slice(c * FCHUNK, (c + 1) * FCHUNK)
        act, slope = gelu_pair(mm(normed, w_up[:, at]) + hid_bias[1:2, at])
        act = act.astype(BF)
        act_out[:, at] = act
        slope_keep[:, at] = slope.astype(BF)
        total = total + mm(act, w_down[at, :])
    latents[...] = total.astype(BF)
    grad_low = grad[...]
    mlp_back(first, grad_low, grad_low.astype(F32), slope_keep, xhat, rstd, norms[6:7, :], w_up, w_down, g3, dpre_out, dnorm, dhid, dout)


def mlp_back(first, grad_low, grad_rows, slope, xhat, rstd, gain, w_up, w_down, grad_out, dpre_out, dnorm, dhid, dout):
    grad_normed = jnp.zeros(grad_rows.shape, F32)
    for c in range(FF // FCHUNK):
        at = slice(c * FCHUNK, (c + 1) * FCHUNK)
        dpre = (mm_t(grad_low, w_down[at, :]) * slope[:, at].astype(F32)).astype(BF)
        dpre_out[:, at] = dpre
        part = col_sum(dpre.astype(F32))

        @pl.when(first)
        def _(at=at, part=part):
            dhid[:, at] = part

        @pl.when(jnp.logical_not(first))
        def _(at=at, part=part):
            dhid[:, at] += part

        grad_normed = grad_normed + mm_t(dpre, w_up[:, at])
    accumulate(first, dnorm, jnp.concatenate([col_sum(grad_normed * xhat), col_sum(grad_normed)], axis=0))
    accumulate(first, dout, col_sum(grad_low.astype(F32)))
    grad_out[...] = grad_rows + norm_back(grad_normed, xhat, rstd, gain)


def mlp_one_bwd_kernel(h1, g2, slope, norms, w_up, w_down, g1, low_out, dpre_out, dnorm, dhid, dout):
    first = pl.program_id(0) == 0
    xhat, rstd = norm_stats(h1[...])
    grad_rows = g2[...]
    grad_low = grad_rows.astype(BF)
    low_out[...] = grad_low
    mlp_back(first, grad_low, grad_rows, slope, xhat, rstd, norms[2:3, :], w_up, w_down, g1, dpre_out, dnorm, dhid, dout)


def self_fwd_kernel(qkv, h2, w_so, out_bias, h3, mixed_out, lse_out):
    scale = jnp.asarray(0.125, BF)
    mixed_rows = []
    for pair in range(HEADS // 2):
        base = pair * LANES
        query_pair = qkv[:, base : base + LANES] * scale
        key_pair = qkv[:, D + base : D + base + LANES]
        value_t = qkv[:, 2 * D + base : 2 * D + base + LANES].T
        for half in range(2):
            scores = mm_t(key_pair, keep_half(query_pair, half))
            top = jnp.max(scores, axis=0, keepdims=True)
            terms = jnp.exp(scores - top)
            total = jnp.sum(terms, axis=0, keepdims=True)
            prob = (terms * (1.0 / total)).astype(BF)
            head = 2 * pair + half
            lse_out[0, head : head + 1, :] = top + jnp.log(total)
            mixed_rows.append(mm(value_t[half * 64 : half * 64 + 64, :], prob))
    mixed = jnp.concatenate(mixed_rows, axis=0).T.astype(BF)
    mixed_out[...] = mixed
    h3[...] = h2[...] + mm(mixed, w_so[...]) + out_bias[2:3, :]


def self_bwd_kernel(qkv, lse, g3, h2, norms, w_so, w_qkv, g2, low_out, dqkv_out, dnorm, dout):
    first = pl.program_id(0) == 0
    scale = jnp.asarray(0.125, BF)
    grad_rows = g3[...]
    grad_low = grad_rows.astype(BF)
    low_out[...] = grad_low
    accumulate(first, dout, col_sum(grad_low.astype(F32)))
    grad_mixed = mm_t(grad_low, w_so[...]).astype(BF)
    for pair in range(HEADS // 2):
        base = pair * LANES
        query_pair = qkv[:, base : base + LANES] * scale
        key_pair = qkv[:, D + base : D + base + LANES]
        value_pair = qkv[:, 2 * D + base : 2 * D + base + LANES]
        grad_pair = grad_mixed[:, base : base + LANES]
        key_t = key_pair.T
        query_t = []
        grad_key = jnp.zeros((LAT, LANES), F32)
        grad_value = jnp.zeros((LAT, LANES), F32)
        for half in range(2):
            head = 2 * pair + half
            query = keep_half(query_pair, half)
            grad_head = keep_half(grad_pair, half)
            prob = jnp.exp(mm_t(key_pair, query) - lse[0, head : head + 1, :])
            grad_value = grad_value + mm(prob.astype(BF), grad_head)
            weighted = prob * mm_t(value_pair, grad_head)
            grad_score = (weighted - prob * col_sum(weighted)).astype(BF)
            grad_key = grad_key + mm(grad_score, query)
            query_t.append(mm(key_t[half * 64 : half * 64 + 64, :], grad_score))
        dqkv_out[:, base : base + LANES] = (jnp.concatenate(query_t, axis=0).T * 0.125).astype(BF)
        dqkv_out[:, D + base : D + base + LANES] = grad_key.astype(BF)
        dqkv_out[:, 2 * D + base : 2 * D + base + LANES] = grad_value.astype(BF)
    grad_in = mm_t(dqkv_out[...], w_qkv[...])
    xhat, rstd = norm_stats(h2[...])
    accumulate(first, dnorm, jnp.concatenate([col_sum(grad_in * xhat), col_sum(grad_in)], axis=0))
    g2[...] = grad_rows + norm_back(grad_in, xhat, rstd, norms[4:5, :])


def segment_hot(starts, ends, base, rows):
    row = lax.broadcasted_iota(jnp.int32, (16, rows), 1) + base
    return jnp.where((row >= starts[:, 0:1]) & (row < ends[:, 0:1]), 1.0, 0.0).astype(BF)


def segment_sums(hot, squares):
    high = squares.astype(BF)
    low = (squares - high.astype(F32)).astype(BF)
    return mm(hot, high) + mm(hot, low)


def grad_stats_kernel(base, starts, ends, summed, master, grad_out, grad_sq, weight_sq):
    i = pl.program_id(0)
    rows = master.shape[0]
    hot = segment_hot(starts, ends, base[0] + i * rows, rows)
    grad = summed[...].astype(F32)
    grad_out[...] = grad
    accumulate(i == 0, grad_sq, col_sum(grad * grad))
    accumulate(i == 0, weight_sq, segment_sums(hot, master[...] * master[...]))


def lamb_kernel(base, clip, starts, ends, grad, master, one, two, update_out, one_out, two_out, update_sq):
    i = pl.program_id(0)
    rows = master.shape[0]
    hot = segment_hot(starts, ends, base[0] + i * rows, rows)
    clipped = clip[0] * grad[...]
    new_one = beta_one * one[...] + (1.0 - beta_one) * clipped
    new_two = beta_two * two[...] + (1.0 - beta_two) * clipped * clipped
    one_out[...] = new_one
    two_out[...] = new_two
    first_hat = new_one * (1.0 / (1.0 - beta_one**lamb_step))
    second_hat = new_two * (1.0 / (1.0 - beta_two**lamb_step))
    update = first_hat / (jnp.sqrt(second_hat) + adam_eps) + decay_rate * master[...]
    update_out[...] = update
    accumulate(i == 0, update_sq, segment_sums(hot, update * update))


def fixed(*shape):
    return pl.BlockSpec(shape, lambda i: (0,) * len(shape), pipeline_mode=pl.Buffered(1))


def kept(*shape):
    return pl.BlockSpec(shape, lambda i: (0,) * len(shape))


def rowed(rows, cols):
    return pl.BlockSpec((rows, cols), lambda i: (i, 0))


def framed(*shape):
    return pl.BlockSpec((1,) + shape, lambda i: (i,) + (0,) * len(shape))


def shaped(shape, dtype=F32):
    return jax.ShapeDtypeStruct(shape, dtype)


def call(kernel, grid, in_specs, outs, args, flops=0, trans=0, scratch=(), limit=56):
    out_specs, out_shapes = zip(*outs)
    moved = sum(math.prod(a.shape) * a.dtype.itemsize for a in args)
    moved += sum(math.prod(s.shape) * s.dtype.itemsize for s in out_shapes)
    return pl.pallas_call(
        kernel,
        grid=(grid,),
        in_specs=in_specs,
        out_specs=list(out_specs),
        out_shape=list(out_shapes),
        scratch_shapes=list(scratch),
        compiler_params=pltpu.CompilerParams(
            dimension_semantics=("arbitrary",), vmem_limit_bytes=limit * MIB
        ),
        cost_estimate=pl.CostEstimate(flops=flops, bytes_accessed=moved, transcendentals=trans),
    )(*args)


def body(tokens, frame_ids, episodes, master, moment_one, moment_two, latent_grad):
    lat_count = lax.axis_size("lat")
    lat_index = lax.axis_index("lat")
    shard_len = master.shape[0]
    frame_total = episodes.shape[1]
    frames = frame_total // lat_count
    rows_total = frames * LAT
    total_keys = frame_ids.shape[1] * lat_count
    cap = total_keys // 8
    token_rows_count = total_keys // LANES

    grad_rows_in = lax.all_to_all(
        latent_grad[0], "lat", split_axis=0, concat_axis=1, tiled=True
    ).reshape(rows_total, D)

    whole_flat = lax.all_gather(master.astype(BF), "lat", axis=0, tiled=True)
    weights = split_flat(whole_flat)
    norms = weights["lat_norms"].astype(F32)
    out_bias = weights["out_bias"].astype(F32)
    hid_bias = weights["hid_bias"].astype(F32)
    tok_norm = weights["tok_norm"].astype(F32)

    frame_tag = lax.all_gather(frame_ids[0].astype(BF), "lat", axis=0, tiled=True).astype(jnp.int32)
    own_frames = lat_index * frames + jnp.arange(frames, dtype=jnp.int32)
    own_hit = frame_tag[None, :] == own_frames[:, None]
    rank = jnp.cumsum(own_hit.astype(jnp.int32), axis=1) - 1
    counts = jnp.broadcast_to(rank[:, -1][:, None, None] + 1, (frames, 8, LANES))
    rank = jnp.where(own_hit, rank, -1).reshape(frames, token_rows_count, LANES)

    token_values = tokens[0].astype(F32)
    tok_full, token_pull = jax.vjp(layer_norm, token_values, tok_norm[0], tok_norm[1])
    tok_normed = tok_full.astype(BF)
    key_value = mm(tok_normed, weights["w_kv"]).astype(BF)
    all_keys = lax.all_gather(key_value, "lat", axis=0, tiled=True)

    episode_index = jnp.arange(EPISODES, dtype=jnp.int32)
    own_episodes = lax.dynamic_slice_in_dim(episodes[0], lat_index * frames, frames, 0)
    episode_match = own_episodes[:, None] == episode_index[None, :]
    episode_rows = mm(episode_match.astype(BF), weights["episode"]).reshape(frames, 1, D)
    w_q = jnp.pad(weights["w_q"], ((0, 0), (0, LANES - CH)))
    w_o = jnp.pad(weights["w_o"], ((LANES - CH, 0), (0, 0)))
    latent = weights["latent"]

    score_flops = rows_total * cap * LANES * 2
    select_flops = frames * cap * total_keys * LANES * 2
    h1, kvf, cross_out, cross_lse = call(
        cross_fwd_kernel,
        frames,
        [
            fixed(LAT, D), framed(1, D), fixed(8, D), fixed(D, LANES), fixed(LANES, D), fixed(4, D),
            fixed(total_keys, LANES), framed(token_rows_count, LANES), framed(8, LANES),
        ],
        [
            (rowed(LAT, D), shaped((rows_total, D))),
            (framed(cap, LANES), shaped((frames, cap, LANES), BF)),
            (rowed(LAT, LANES), shaped((rows_total, LANES), BF)),
            (framed(1, LAT), shaped((frames, 1, LAT))),
        ],
        (latent, episode_rows, norms, w_q, w_o, out_bias, all_keys, rank, counts),
        flops=2 * score_flops + select_flops,
        trans=rows_total * cap,
    )

    block = min(512, rows_total)
    steps = rows_total // block
    mlp_flops = 4 * rows_total * D * FF
    h2, normed_one, act_one, slope_one, sa_in, qkv = call(
        mlp_one_fwd_kernel,
        steps,
        [rowed(block, D), fixed(8, D), fixed(2, FF), fixed(4, D), fixed(D, FF), fixed(FF, D), fixed(D, 3 * D)],
        [
            (rowed(block, D), shaped((rows_total, D))),
            (rowed(block, D), shaped((rows_total, D), BF)),
            (rowed(block, FF), shaped((rows_total, FF), BF)),
            (rowed(block, FF), shaped((rows_total, FF), BF)),
            (rowed(block, D), shaped((rows_total, D), BF)),
            (rowed(block, 3 * D), shaped((rows_total, 3 * D), BF)),
        ],
        (h1, norms, hid_bias, out_bias, weights["w_up"][0], weights["w_down"][0], weights["w_qkv"]),
        flops=mlp_flops + 6 * rows_total * D * D,
        trans=2 * rows_total * FF,
    )

    attn_flops = 4 * rows_total * LAT * D
    h3, mixed, self_lse = call(
        self_fwd_kernel,
        frames,
        [rowed(LAT, 3 * D), rowed(LAT, D), fixed(D, D), fixed(4, D)],
        [
            (rowed(LAT, D), shaped((rows_total, D))),
            (rowed(LAT, D), shaped((rows_total, D), BF)),
            (framed(HEADS, LAT), shaped((frames, HEADS, LAT))),
        ],
        (qkv, h2, weights["w_so"], out_bias),
        flops=4 * attn_flops,
        trans=rows_total * LAT * HEADS,
    )

    latents, g3, normed_two, act_two, dpre_two, dnorm_two, dhid_two, dout_two = call(
        mlp_two_kernel,
        steps,
        [rowed(block, D), rowed(block, D), fixed(8, D), fixed(2, FF), fixed(4, D), fixed(D, FF), fixed(FF, D)],
        [
            (rowed(block, D), shaped((rows_total, D), BF)),
            (rowed(block, D), shaped((rows_total, D))),
            (rowed(block, D), shaped((rows_total, D), BF)),
            (rowed(block, FF), shaped((rows_total, FF), BF)),
            (rowed(block, FF), shaped((rows_total, FF), BF)),
            (kept(2, D), shaped((2, D))),
            (kept(1, FF), shaped((1, FF))),
            (kept(1, D), shaped((1, D))),
        ],
        (h3, grad_rows_in, norms, hid_bias, out_bias, weights["w_up"][1], weights["w_down"][1]),
        flops=2 * mlp_flops,
        trans=2 * rows_total * FF,
        scratch=[pltpu.VMEM((block, FF), BF)],
    )
    latents_out = lax.all_to_all(
        latents.reshape(frames, LAT, D), "lat", split_axis=1, concat_axis=0, tiled=True
    )[None]
    two_down = t_mm(act_two, grad_rows_in)
    two_up = t_mm(normed_two, dpre_two)

    g2, low_three, dqkv, dnorm_sa, dout_so = call(
        self_bwd_kernel,
        frames,
        [
            rowed(LAT, 3 * D), framed(HEADS, LAT), rowed(LAT, D), rowed(LAT, D), fixed(8, D),
            fixed(D, D), fixed(D, 3 * D),
        ],
        [
            (rowed(LAT, D), shaped((rows_total, D))),
            (rowed(LAT, D), shaped((rows_total, D), BF)),
            (rowed(LAT, 3 * D), shaped((rows_total, 3 * D), BF)),
            (kept(2, D), shaped((2, D))),
            (kept(1, D), shaped((1, D))),
        ],
        (qkv, self_lse, g3, h2, norms, weights["w_so"], weights["w_qkv"]),
        flops=10 * attn_flops,
        trans=rows_total * LAT * HEADS,
    )
    grad_so = t_mm(mixed, low_three)
    grad_qkv = t_mm(sa_in, dqkv)

    g1, low_two, dpre_one, dnorm_one, dhid_one, dout_one = call(
        mlp_one_bwd_kernel,
        steps,
        [rowed(block, D), rowed(block, D), rowed(block, FF), fixed(8, D), fixed(D, FF), fixed(FF, D)],
        [
            (rowed(block, D), shaped((rows_total, D))),
            (rowed(block, D), shaped((rows_total, D), BF)),
            (rowed(block, FF), shaped((rows_total, FF), BF)),
            (kept(2, D), shaped((2, D))),
            (kept(1, FF), shaped((1, FF))),
            (kept(1, D), shaped((1, D))),
        ],
        (h1, g2, slope_one, norms, weights["w_up"][0], weights["w_down"][0]),
        flops=mlp_flops,
    )
    one_down = t_mm(act_one, low_two)
    one_up = t_mm(normed_one, dpre_one)

    grad_latent, frame_sums, dnorm_q, dw_q, dw_o, dout_cross, dkv_t = call(
        cross_bwd_kernel,
        frames,
        [
            fixed(LAT, D), framed(1, D), fixed(8, D), fixed(D, LANES), fixed(LANES, D),
            framed(cap, LANES), rowed(LAT, LANES), framed(1, LAT), framed(token_rows_count, LANES),
            framed(8, LANES), rowed(LAT, D),
        ],
        [
            (kept(LAT, D), shaped((LAT, D))),
            (framed(1, D), shaped((frames, 1, D))),
            (kept(2, D), shaped((2, D))),
            (kept(D, LANES), shaped((D, LANES))),
            (kept(LANES, D), shaped((LANES, D))),
            (kept(1, D), shaped((1, D))),
            (kept(LANES, total_keys), shaped((LANES, total_keys))),
        ],
        (latent, episode_rows, norms, w_q, w_o, kvf, cross_out, cross_lse, rank, counts, g1),
        flops=5 * score_flops + select_flops,
        trans=rows_total * cap,
    )
    grad_episode = jnp.sum(episode_match.astype(F32)[:, :, None] * frame_sums, axis=0)

    grad_kv = lax.psum_scatter(dkv_t.T.astype(BF), "lat", scatter_dimension=0, tiled=True)
    grad_w_kv = t_mm(tok_normed, grad_kv)
    grad_tok_normed = mm_t(grad_kv, weights["w_kv"])
    grad_tokens, grad_tok_gain, grad_tok_bias = token_pull(grad_tok_normed)
    token_grad = grad_tokens.astype(BF)[None]

    grads = {
        "latent": grad_latent,
        "episode": grad_episode,
        "tok_norm": jnp.stack([grad_tok_gain, grad_tok_bias]),
        "lat_norms": jnp.concatenate([dnorm_q, dnorm_one, dnorm_sa, dnorm_two]),
        "w_kv": grad_w_kv,
        "w_q": dw_q[:, :CH],
        "w_o": dw_o[LANES - CH :],
        "w_qkv": grad_qkv,
        "w_so": grad_so,
        "w_up": jnp.stack([one_up, two_up]),
        "w_down": jnp.stack([one_down, two_down]),
        "hid_bias": jnp.concatenate([dhid_one, dhid_two]),
        "out_bias": jnp.concatenate([dout_cross, dout_one, dout_so, dout_two]),
    }
    layout = param_layout()
    local_flat = jnp.concatenate([grads[name].astype(BF).reshape(-1) for name, unused in layout])
    summed = lax.psum_scatter(local_flat, "lat", scatter_dimension=0, tiled=True)
    summed = lax.psum(summed, "kf")

    starts, ends, offset, bias_offset = [], [], 0, 0
    for name, shape in layout:
        if name == "hid_bias":
            bias_offset = offset
        starts.append(offset // LANES)
        offset += math.prod(shape)
        ends.append(offset // LANES)
    pad = [0] * (16 - len(layout))
    starts = jnp.broadcast_to(jnp.array(starts + pad, jnp.int32)[:, None], (16, LANES))
    ends = jnp.broadcast_to(jnp.array(ends + pad, jnp.int32)[:, None], (16, LANES))
    shard_rows = shard_len // LANES
    opt_rows = 784 if shard_rows % 784 == 0 else shard_rows
    opt_steps = shard_rows // opt_rows
    base = (lat_index * shard_rows).astype(jnp.int32).reshape(1)
    smem = pl.BlockSpec(memory_space=pltpu.SMEM)
    flat_rows = (shard_rows, LANES)
    master_rows = master.reshape(flat_rows)
    grad_shard, grad_sq, weight_sq = call(
        grad_stats_kernel,
        opt_steps,
        [smem, fixed(16, LANES), fixed(16, LANES), rowed(opt_rows, LANES), rowed(opt_rows, LANES)],
        [
            (rowed(opt_rows, LANES), shaped(flat_rows)),
            (kept(1, LANES), shaped((1, LANES))),
            (kept(16, LANES), shaped((16, LANES))),
        ],
        (base, starts, ends, summed.reshape(flat_rows), master_rows),
    )
    bias_owner, bias_at = divmod(bias_offset, shard_len)
    bias_part = jnp.where(
        lat_index == bias_owner, grad_shard.reshape(-1)[bias_at : bias_at + 2 * FF], 0.0
    )
    total_sq, weight_sq, bias_total = lax.psum(
        (jnp.sum(grad_sq), jnp.sum(weight_sq, axis=1), bias_part), "lat"
    )
    bias_grad = bias_total.reshape(2, FF)
    clip_scale = jnp.minimum(1.0, clip_fraction * math.sqrt(NPARAM) / (jnp.sqrt(total_sq) + 1e-06))
    lamb_update, new_one, new_two, update_sq = call(
        lamb_kernel,
        opt_steps,
        [smem, smem, fixed(16, LANES), fixed(16, LANES)] + [rowed(opt_rows, LANES)] * 4,
        [(rowed(opt_rows, LANES), shaped(flat_rows))] * 3 + [(kept(16, LANES), shaped((16, LANES)))],
        (
            base, clip_scale.reshape(1), starts, ends, grad_shard, master_rows,
            moment_one.reshape(flat_rows), moment_two.reshape(flat_rows),
        ),
    )
    update_sq = lax.psum(jnp.sum(update_sq, axis=1), "lat")
    trust = (jnp.sqrt(weight_sq) / (jnp.sqrt(update_sq) + 1e-06))[: len(layout)]
    return (
        latents_out,
        token_grad,
        grad_shard.reshape(-1),
        lamb_update.reshape(-1),
        new_one.reshape(-1),
        new_two.reshape(-1),
        trust,
        bias_grad,
    )


def solution(mesh):
    return jax.shard_map(
        body,
        mesh=mesh,
        in_specs=(
            P("kf", "lat", None),
            P("kf", "lat"),
            P("kf", None),
            P("lat"),
            P("lat"),
            P("lat"),
            P("kf", None, "lat", None),
        ),
        out_specs=(
            P("kf", None, "lat", None),
            P("kf", "lat", None),
            P("lat"),
            P("lat"),
            P("lat"),
            P("lat"),
            P(),
            P(),
        ),
        check_vma=False,
    )
```

time: 1190 us -> 722 us (0.61)
  matrix products: 383 us -> 48.8 us
  Pallas kernels: 0 us -> 208 us
  waiting for transfers between devices: 433 us -> 254 us
  local copies, waits for them, and re-layouts: 193 us -> 77.1 us
  other arithmetic: 93.4 us -> 18.3 us
  blocking collectives: 47.3 us -> 81.6 us
    dot_general x70 -> x10, matrix products: 383 us -> 48.8 us  [the longest x7 44.9 us: t_mm(): lax.dot_general(left, right, (((0,), (0,)), ((), ())), preferred_element_...]
    pallas_call x0 -> x9, Pallas kernels: none -> 208 us  [call(): pl.pallas_call(kernel, grid=(grid,), in_specs=in_specs, out_specs=list(ou...]
    all_to_all x4 -> x2, waiting for transfers between devices: 162 us -> 0.01 us  [the longest x1 0.01 us: body(): lax.all_to_all(latent_grad[0], 'lat', split_axis=0, concat_axis=1, tiled=...]
    reduce_sum x19 -> x4, other arithmetic: 53.4 us -> 3.02 us  [the longest x1 1.26 us: body(): jnp.sum(grad_sq)]
    all_gather x1, blocking collectives: 10.4 us -> 44.7 us  [body(): lax.all_gather(frame_ids[0].astype(BF), 'lat', axis=0, tiled=True)]
    all_gather x2, waiting for transfers between devices: 58.4 us -> 29.1 us  [the longest x1 29.1 us: body(): whole_flat = lax.all_gather(master.astype(BF), 'lat', axis=0, tiled=True)]
    while x17 -> x0, local copies, waits for them, and re-layouts: 26.5 us -> none  [the longest x2 13.7 us: self_mix(): self_acc, self_total = lax.map(self_forward, qkv_frames)]
    gather x1 -> x0, local copies, waits for them, and re-layouts: 23 us -> none  [body(): grad_shard[jnp.clip(bias_local, 0, shard_len - 1)]]
  transfers between devices with their start and end apart: 9 -> 7, of which waited for: 8 -> 4; matrix products, arithmetic and copies ran while one was open for 8% -> 10% of each run, Pallas kernels for 0% -> 3%
where the time goes in v1:
time: 722 us; the launch traced here: 713 us
  waiting for transfers between devices  254 us (35%)
  Pallas kernels  208 us (29%)
  blocking collectives  81.6 us (11%)
  local copies, waits for them, and re-layouts  77.1 us (11%)
  matrix products  48.8 us (7%)
  other arithmetic  18.3 us (3%)
  between operations  16.3 us (2%)
  starting transfers between devices  9.68 us (1%)
    pallas_call x9, Pallas kernels, call(): pl.pallas_call(kernel, grid=(grid,), in_specs=in_specs, out_specs=list(ou...  208 us
    unnamed x6, waiting for transfers between devices  156 us
    psum x1, waiting for transfers between devices, body(): summed = lax.psum(summed, 'kf')  56.4 us
    dot_general x7, matrix products, t_mm(): lax.dot_general(left, right, (((0,), (0,)), ((), ())), preferred_element_...  44.9 us
    all_gather x1, blocking collectives, body(): lax.all_gather(frame_ids[0].astype(BF), 'lat', axis=0, tiled=True)  44.7 us
    all_gather x1, waiting for transfers between devices, body(): whole_flat = lax.all_gather(master.astype(BF), 'lat', axis=0, tiled=True)  29.1 us
    unnamed x109, local copies, waits for them, and re-layouts  28.1 us
    psum x1, blocking collectives, body(): update_sq = lax.psum(jnp.sum(update_sq, axis=1), 'lat')  22.9 us
  transfers between devices with their start and end apart: 7, of which 4 were waited for; matrix products, arithmetic and copies ran while one was open for 10% of the time, Pallas kernels for 3%

profile of v1, /device:TPU:0, one launch (start us, length us, event | category | flops | bytes accessed | tf_op | source)
XLA Modules:
  0.0 713.4 jit_solution(3662753664349448002)
XLA Ops:
  7.2 3.0 convert_element_type.117
  10.3 5.3 all-to-all-start
  15.7 44.7 %all-gather = bf16[1,4096]{1,0:T(2,128)(2,1)S(1)} all-gather(bf16[1,512]{1,0:T(2,128)(2,1)S(1)} %convert_element_type.127), channel_id=2, replica_groups=mesh['kf'=4,'lat'=8] {'lat'}, dimensions={1}, use_global_device_ids=true | all-gather | bytes 9216 | tf_op jit(solution)/shard_map/all_gather | solution.py:454
  62.7 2.0 copy.31
  65.9 1.5 copy.28
  67.5 29.1 %all-gather.4.cloned.1.call-done = bf16[5619712]{0:T(1024)(128)(2,1)} async-done(((bf16[702464]{0:T(1024)(128)(2,1)}), bf16[5619712]{0:T(1024)(128)(2,1)}) %all-gather.4.cloned.1.call-update) | async-done | bytes 11239440 | tf_op jit(solution)/shard_map/all_gather | solution.py:447
  97.3 1.8 convolution_convert_fusion.6
  99.8 6.6 fusion.30
  106.3 3.1 copy-done.4
  117.5 2.7 reshape.366.w_qkv
  120.2 4.4 slice.254.w_down
  124.6 4.5 slice.247.w_down
  129.1 4.2 slice.245.w_up
  133.2 2.3 slice.252.w_up
  136.2 16.1 %shard_map.152 = (f32[2048,512]{1,0:T(8,128)}, bf16[4,512,128]{2,1,0:T(8,128)(2,1)}, bf16[2048,128]{1,0:T(8,128)(2,1)}, f32[4,1,512]{2,1,0:T(1,128)}) custom-call(bf16[512,512]{1,0:T(8,128)(2,1)} %slice.226.latent, f32[4,1,512]{2,1,0:T(1,128)} %reshape.364.episode, f32[8,512]{1,0:T(8,128)} %reshape.389.norms, bf16[512,128]{1,0:T(8,128)(2,1)} %pad.8.w_q, ...), custom_call_target="tpu_custom_call" | custom-call | flops 2684354560 | bytes 7200768 | tf_op jit(solution)/shard_map/pallas_call | solution.py:418
  152.3 31.0 %shard_map.153 = (f32[2048,512]{1,0:T(8,128)}, bf16[2048,512]{1,0:T(8,128)(2,1)}, bf16[2048,2048]{1,0:T(8,128)(2,1)}, bf16[2048,2048]{1,0:T(8,128)(2,1)}, bf16[2...) custom-call(f32[2048,512]{1,0:T(8,128)} %get-tuple-element.54.h1, f32[8,512]{1,0:T(8,128)} %reshape.389.norms, ...), custom_call_target="tpu_custom_call" | custom-call | flops 11811160064 | bytes 41459712 | tf_op jit(solution)/shard_map/pallas_call | solution.py:418
  183.3 22.4 %shard_map.154 = (f32[2048,512]{1,0:T(8,128)}, bf16[2048,512]{1,0:T(8,128)(2,1)}, f32[4,8,512]{2,1,0:T(8,128)}) custom-call(bf16[2048,1536]{1,0:T(8,128)(2,1)} %get-tuple-element.55.qkv, f32[2048,512]{1,0:T(8,128)} %get-tuple-element.56.h2, bf16[512,512]{1,0:T(8,128)(2,1)} %slice.250.w_so, f32[4,512]{1,0:T(4,128)} %reshape.390.out_bias), custom_call_target="tpu_custom_call" | custom-call | flops 8589934592 | bytes 17375232 | tf_op jit(solution)/shard_map/pallas_call | solution.py:418
  205.7 41.3 %shard_map.155 = (bf16[2048,512]{1,0:T(8,128)(2,1)}, f32[2048,512]{1,0:T(8,128)}, bf16[2048,512]{1,0:T(8,128)(2,1)}, bf16[2048,2048]{1,0:T(8,128)(2,1)}, bf16[20...) custom-call(f32[2048,512]{1,0:T(8,128)} %get-tuple-element.57.h3, ...), custom_call_target="tpu_custom_call" | custom-call | flops 17179869184 | bytes 35706880 | tf_op jit(solution)/shard_map/pallas_call | solution.py:418
  247.0 9.5 %fusion.3 = bf16[1,2048,512]{2,1,0:T(8,128)(2,1)} fusion(bf16[2048,2048]{1,0:T(8,128)(2,1)} %get-tuple-element.86, bf16[2048,512]{1,0:T(8,128)(2,1)S(1)} %bitcast.140), kind=kOutput, calls=%fused_computation.10 | convolution fusion | flops 4296015872 | bytes 12582912 | tf_op jit(solution)/shard_map/dot_general | solution.py:80
  256.5 36.3 %shard_map.156 = (f32[2048,512]{1,0:T(8,128)}, bf16[2048,512]{1,0:T(8,128)(2,1)}, bf16[2048,1536]{1,0:T(8,128)(2,1)}, f32[2,512]{1,0:T(2,128)}, f32[1,512]{1,0:T(1,128)}) custom-call(bf16[2048,1536]{1,0:T(8,128)(2,1)} %get-tuple-element.55.qkv, f32[4,8,512]{2,1,0:T(8,128)} %get-tuple-element.62.lse, f32[2048,512]{1,0:T(8,128)} %get-tuple-element.63.g3, ...), custom_call_target="tpu_custom_call" | custom-call | flops 21474836480 | bytes 29448192 | tf_op jit(solution)/shard_map/pallas_call | solution.py:418
  292.8 3.0 fusion.4
  296.1 7.3 %convolution_convert_fusion.4 = bf16[512,1536]{1,0:T(8,128)(2,1)} fusion(bf16[2048,512]{1,0:T(8,128)(2,1)S(1)} %copy-done.39, bf16[2048,1536]{1,0:T(8,128)(2,1)} %get-tuple-element.77), kind=kOutput, calls=%fused_computation.6 | convolution fusion | flops 3222011904 | bytes 9961472 | tf_op jit(solution)/shard_map/dot_general | solution.py:80
  303.4 3.3 reshape.376
  306.7 21.9 %shard_map.157 = (f32[2048,512]{1,0:T(8,128)}, bf16[2048,512]{1,0:T(8,128)(2,1)}, bf16[2048,2048]{1,0:T(8,128)(2,1)}, f32[2,512]{1,0:T(2,128)}, f32[1,2048]{1,0:T(1,128)}, /*index=5*/f32[1,512]{1,0:T(1,128)}) custom-call(f32[2048,512]{1,0:T(8,128)} %get-tuple-element.54.h1, f32[2048,512]{1,0:T(8,128)} %get-tuple-element.64.g2, ...), custom_call_target="tpu_custom_call" | custom-call | flops 8589934592 | bytes 35682304 | tf_op jit(solution)/shard_map/pallas_call | solution.py:418
  328.7 8.7 %fusion.2 = bf16[1,2048,512]{2,1,0:T(8,128)(2,1)S(1)} fusion(bf16[2048,2048]{1,0:T(8,128)(2,1)} %get-tuple-element.84, bf16[2048,512]{1,0:T(8,128)(2,1)} %get-tuple-element.85), kind=kOutput, calls=%fused_computation.9 | convolution fusion | flops 4296015872 | bytes 12582912 | tf_op jit(solution)/shard_map/dot_general | solution.py:80
  337.8 4.1 copy.39
  341.9 20.9 %shard_map.158 = (f32[512,512]{1,0:T(8,128)}, f32[4,1,512]{2,1,0:T(1,128)}, f32[2,512]{1,0:T(2,128)}, f32[512,128]{1,0:T(8,128)}, f32[128,512]{1,0:T(8,128)}, /*index=5*/f32[1,512]{1,0:T(1,128)}, f32[128,4096]{1,0:T(8,128)}) custom-call(bf16[512,512]{1,0:T(8,128)(2,1)} %slice.226.latent, f32[4,1,512]{2,1,0:T(1,128)} %reshape.364.episode, ...), custom_call_target="tpu_custom_call" | custom-call | flops 3489660928 | bytes 9828352 | tf_op jit(solution)/shard_map/pallas_call | solution.py:418
  362.9 2.7 convert_bitcast_fusion
  367.9 1.5 convert_bitcast_fusion.2
  370.4 8.9 %fusion = bf16[1,512,2048]{2,1,0:T(8,128)(2,1)S(1)} fusion(bf16[2048,512]{1,0:T(8,128)(2,1)} %get-tuple-element.80, bf16[2048,2048]{1,0:T(8,128)(2,1)} %get-tuple-element.81), kind=kOutput, calls=%fused_computation.7 | convolution fusion | flops 4296015872 | bytes 12582912 | tf_op jit(solution)/shard_map/dot_general | solution.py:80
  379.4 5.1 fusion.1
  385.0 3.4 copy.38
  388.4 1.5 dynamic-update-slice.1
  389.9 12.0 %reduce-scatter.2.cloned.1.call-done = bf16[512,128]{0,1:T(8,128)(2,1)} async-done(((bf16[4096,128]{0,1:T(8,128)(2,1)}), bf16[512,128]{0,1:T(8,128)(2,1)}) %reduce-scatter.2.cloned.1.call-update) | async-done | bytes 131088 | tf_op jit(solution)/shard_map/reduce_scatter | solution.py:617
  401.9 1.9 fusion.16
  405.8 2.3 fusion.6
  411.5 2.3 constant_dynamic-update-slice_fusion.3
  415.2 2.2 constant_dynamic-update-slice_fusion.2
  420.5 156.1 %all-reduce.9.cloned.1.call-done = bf16[5619712]{0:T(1024)(128)(2,1)} async-done(((bf16[5619712]{0:T(1024)(128)(2,1)}), bf16[5619712]{0:T(1024)(128)(2,1)}) %all-reduce.9.cloned.1.call-update) | async-done | bytes 11239440
  576.5 2.5 dynamic-slice_bitcast_fusion
  579.1 2.9 copy.29
  582.1 3.6 all-to-all-start.1
  586.2 56.4 %all-reduce.7.cloned.1.call-done.summed = bf16[5488,128]{1,0:T(8,128)(2,1)} async-done(((bf16[5488,128]{1,0:T(8,128)(2,1)}), bf16[5488,128]{1,0:T(8,128)(2,1)}) %all-reduce.7.cloned.1.call-update) | async-done | bytes 1404944 | tf_op jit(solution)/shard_map/psum | solution.py:641
  643.9 7.0 shard_map.159
  653.0 14.0 %psum.36 = f32[]{:T(128)} all-reduce(f32[]{:T(128)} %reduce_sum.113), channel_id=1, replica_groups=mesh['kf'=4,'lat'=8] {'lat'}, use_global_device_ids=true, to_apply=%region_13.14 | all-reduce | flops 1 | bytes 8 | tf_op jit(solution)/shard_map/psum | solution.py:675
  669.3 11.2 %shard_map.160 = (f32[5488,128]{1,0:T(8,128)}, f32[5488,128]{1,0:T(8,128)}, f32[5488,128]{1,0:T(8,128)}, f32[16,128]{1,0:T(8,128)}) custom-call(s32[1]{0:T(128)} %bitcast.16.base, f32[1]{0:T(128)} %bitcast.26.clip, s32[16,128]{1,0:T(8,128)} %broadcast_in_dim.24.starts, s32[16,128]{1,0:T(8,128)} %broadcast_in_dim.48.ends, ...), custom_call_target="tpu_custom_call" | custom-call | bytes 19693576 | tf_op jit(solution)/shard_map/pallas_call | solution.py:418
  681.3 1.8 copy.30
  683.2 22.9 %all-reduce.3 = (f32[16]{0:T(128)S(1)}, f32[16]{0:T(128)S(1)}, f32[2,2048]{1,0:T(2,128)}) all-reduce(f32[16]{0:T(128)S(1)} %reduce_sum.115, f32[16]{0:T(128)S(1)} %reduce_sum.114, f32[2,2048]{1,0:T(2,128)S(1)} %reshape.387), channel_id=1, replica_groups=mesh['kf'=4,'lat'=8] {'lat'}, use_global_device_ids=true, to_apply=%region_17.18 | all-reduce | flops 4128 | bytes 33024 | tf_op jit(solution)/shard_map/psum | solution.py:690
  (190 shorter events, 33.9 us)
Async XLA Ops:
  7.2 57.6 %copy-start = (s32[1,32]{1,0:T(1,128)S(1)}, s32[1,32]{1,0:T(1,128)}, u32[]{:S(2)}) copy-start(s32[1,32]{1,0:T(1,128)} %param.11) | copy-start | bytes 388
  7.2 8.5 %copy-start.29 = (s32[1,512]{1,0:T(1,128)S(1)}, s32[1,512]{1,0:T(1,128)}, u32[]{:S(2)}) copy-start(s32[1,512]{1,0:T(1,128)} %param.10) | copy-start | bytes 6148
  7.2 89.4 %all-gather.4.cloned.1.call-start = ((), (), s32[]{:S(2)}) async-start(), calls=%async_computation.3 | async-start | bytes 12644352 | tf_op jit(solution)/shard_map/all_gather | solution.py:447
  10.3 54.5 %copy-start.6 = (bf16[1,512,256]{2,1,0:T(8,128)(2,1)S(1)}, bf16[1,512,256]{2,1,0:T(8,128)(2,1)}, u32[]{:S(2)}) copy-start(bf16[1,512,256]{2,1,0:T(8,128)(2,1)} %param.9) | copy-start | bytes 786436
  10.3 55.6 %all-to-all-start = ((bf16[32,64,512]{2,1,0:T(8,128)(2,1)}), bf16[32,64,512]{2,1,0:T(8,128)(2,1)S(1)}, u32[]{:S(2)}, u32[]{:S(2)}) async-start(bf16[32,64,512]{2,1,0:T(8,128)(2,1)} %bitcast.137), calls=%async_computation | async-start | bytes 4194304 | tf_op jit(solution)/shard_map/all_to_all | solution.py:443
  15.6 120.0 %all-gather.6.cloned.1.call-start = ((), (), s32[]{:S(2)}) async-start(), calls=%async_computation.4 | async-start | bytes 1179648 | tf_op jit(solution)/shard_map/all_gather | solution.py:465
  65.2 34.5 %copy-start.15 = (f32[512]{0:T(512)}, f32[512]{0:T(512)S(1)}, u32[]{:S(2)}) copy-start(f32[512]{0:T(512)S(1)} %fusion.25) | copy-start | bytes 6148
  97.3 2.5 copy-start.34
  99.1 10.9 %slice-start = ((bf16[5619712]{0:T(1024)(128)(2,1)}), bf16[5632]{0:T(1024)(128)(2,1)S(1)}, s32[]{:S(2)}) async-start(bf16[5619712]{0:T(1024)(128)(2,1)} %all-gather.4.cloned.1.call-done), calls=%async_computation.8 | async-start | bytes 24576 | tf_op jit(solution)/shard_map/slice | solution.py:59
  99.1 302.7 %reduce-scatter.2.cloned.1.call-start = ((), (), s32[]{:S(2)}) async-start(), calls=%async_computation.5 | async-start | bytes 1179648 | tf_op jit(solution)/shard_map/reduce_scatter | solution.py:617
  99.8 9.6 %copy-start.4 = (bf16[5619712]{0:T(1024)(128)(2,1)S(1)}, bf16[5619712]{0:T(1024)(128)(2,1)}, u32[]{:S(2)}) copy-start(bf16[5619712]{0:T(1024)(128)(2,1)} %all-gather.4.cloned.1.call-done) | copy-start | bytes 33718276
  109.4 8.1 %slice-start.1 = ((bf16[5619712]{0:T(1024)(128)(2,1)}), bf16[786432]{0:T(1024)(128)(2,1)S(1)}, s32[]{:S(2)}) async-start(bf16[5619712]{0:T(1024)(128)(2,1)} %all-gather.4.cloned.1.call-done), calls=%async_computation.9 | async-start | bytes 3145728 | tf_op jit(solution)/shard_map/slice | solution.py:59
  124.6 8.6 %copy-start.5 = (bf16[1048576]{0:T(1024)(128)(2,1)S(1)}, bf16[1048576]{0:T(1024)(128)(2,1)}, u32[]{:S(2)}) copy-start(bf16[1048576]{0:T(1024)(128)(2,1)} %get-tuple-element.111) | copy-start | bytes 6291460
  205.7 41.3 %copy-start.8 = (bf16[8,4,64,512]{3,2,0,1:T(8,128)(2,1)S(1)}, bf16[8,4,64,512]{3,2,0,1:T(8,128)(2,1)}, u32[]{:S(2)}) copy-start(bf16[8,4,64,512]{3,2,0,1:T(8,128)(2,1)} %copy.28) | copy-start | bytes 6291460
  256.5 36.3 %copy-start.9 = (bf16[2048,512]{1,0:T(8,128)(2,1)S(1)}, bf16[2048,512]{1,0:T(8,128)(2,1)}, u32[]{:S(2)}) copy-start(bf16[2048,512]{1,0:T(8,128)(2,1)} %get-tuple-element.78) | copy-start | bytes 6291460
  292.8 3.3 copy-start.39
  328.7 8.7 %copy-start.10 = (bf16[1,2048,512]{2,1,0:T(8,128)(2,1)S(1)}, bf16[1,2048,512]{2,1,0:T(8,128)(2,1)}, u32[]{:S(2)}) copy-start(bf16[1,2048,512]{2,1,0:T(8,128)(2,1)} %fusion.3) | copy-start | bytes 6291460
  362.7 2.9 copy-start.24
  362.7 2.9 copy-start.33
  362.8 3.0 copy-start.23
  362.8 3.0 copy-start.32
  362.8 3.0 copy-start.22
  362.8 3.0 copy-start.31
  362.8 3.0 copy-start.21
  362.8 3.1 copy-start.30
  362.8 3.1 copy-start.20
  362.8 3.3 copy-start.19
  362.8 3.3 copy-start.18
  362.8 4.9 copy-start.11
  365.6 210.9 %all-reduce.9.cloned.1.call-start = ((), (), s32[]{:S(2)}) async-start(), calls=%async_computation.7 | async-start | bytes 22478848
  367.9 11.5 %slice-start.2 = ((s8[8388608]{0:T(1024)(128)(4,1)}), s8[4194304]{0:T(1024)(128)(4,1)S(1)}, s32[]{:S(2)}) async-start(s8[8388608]{0:T(1024)(128)(4,1)} %bitcast.158), calls=%async_computation.10 | async-start | bytes 8388608
  370.4 9.0 %slice-start.3 = ((s8[8388608]{0:T(1024)(128)(4,1)}), s8[4194304]{0:T(1024)(128)(4,1)S(1)}, s32[]{:S(2)}) async-start(s8[8388608]{0:T(1024)(128)(4,1)} %bitcast.158), calls=%async_computation.11 | async-start | bytes 8388608
  370.4 9.0 %copy-start.40 = (bf16[2048,512]{1,0:T(8,128)(2,1)S(1)}, bf16[2048,512]{1,0:T(8,128)(2,1)}, u32[]{:S(2)}) copy-start(bf16[2048,512]{1,0:T(8,128)(2,1)} %get-tuple-element.82) | copy-start | bytes 6291460
  384.9 16.9 %copy-start.16 = (f32[512]{0:T(512)S(1)}, f32[512]{0:T(512)}, u32[]{:S(2)}) copy-start(f32[512]{0:T(512)} %copy-done.15) | copy-start | bytes 6148
  384.9 16.9 %copy-start.26 = (f32[256]{0:T(256)S(1)}, f32[256]{0:T(256)}, u32[]{:S(2)}) copy-start(f32[256]{0:T(256)} %copy-done.25) | copy-start | bytes 3076
  385.0 20.9 %copy-start.35 = (f32[256]{0:T(256)S(1)}, f32[256]{0:T(256)}, u32[]{:S(2)}) copy-start(f32[256]{0:T(256)} %copy-done.34) | copy-start | bytes 3076
  405.2 6.3 copy-start.3
  411.5 3.7 copy-start.2
  418.6 160.5 %copy-start.7 = (bf16[2048,512]{1,0:T(8,128)(2,1)S(1)}, bf16[2048,512]{1,0:T(8,128)(2,1)}, u32[]{:S(2)}) copy-start(bf16[2048,512]{1,0:T(8,128)(2,1)} %get-tuple-element.58) | copy-start | bytes 6291460
  418.6 223.9 %all-reduce.7.cloned.1.call-start = ((), (), s32[]{:S(2)}) async-start(), calls=%async_computation.6 | async-start | bytes 2809856 | tf_op jit(solution)/shard_map/psum | solution.py:641
  579.1 6.7 copy-start.14
  579.1 6.7 copy-start.28
  579.1 6.7 copy-start.17
  579.1 6.7 copy-start.27
  579.1 63.4 %copy-start.37 = (s32[16]{0:T(128)S(1)}, s32[16]{0:T(128)}, u32[]{:S(2)}) copy-start(s32[16]{0:T(128)} %constant.49.clone) | copy-start | bytes 196
  579.1 64.1 %copy-start.36 = (s32[16]{0:T(128)S(1)}, s32[16]{0:T(128)}, u32[]{:S(2)}) copy-start(s32[16]{0:T(128)} %constant.50.clone) | copy-start | bytes 196
  582.1 99.2 %all-to-all-start.1 = ((bf16[4,512,512]{2,0,1:T(4,128)(2,1)}), bf16[4,512,512]{2,0,1:T(4,128)(2,1)S(1)}, u32[]{:S(2)}, u32[]{:S(2)}) async-start(bf16[4,512,512]{2,0,1:T(4,128)(2,1)} %copy.29), calls=%async_computation.1 | async-start | bytes 4194304 | tf_op jit(solution)/shard_map/all_to_all | solution.py:549
  669.3 37.3 %copy-start.1 = (s32[1,32]{1,0:T(1,128)S(1)}, s32[1,32]{1,0:T(1,128)}, u32[]{:S(2)}) copy-start(s32[1,32]{1,0:T(1,128)} %param.11) | copy-start | bytes 388
  (4 other events, 6.0 us)
Sparse Core Ops, SparseCore 0:
  10.5 86.0 all-gather.3
  99.3 23.4 all-gather.5
  365.7 36.0 reduce-scatter.1
  418.7 157.7 all-reduce.8
  579.4 63.0 all-reduce.6

commit v2 on v1

--- a/solution.py
+++ b/solution.py
@@ -365,21 +365,24 @@
     return mm(hot, high) + mm(hot, low)
 
 
-def grad_stats_kernel(base, starts, ends, summed, master, grad_out, grad_sq, weight_sq):
+def grad_stats_kernel(base, starts, ends, summed, master, grad_sq, weight_sq):
     i = pl.program_id(0)
     rows = master.shape[0]
     hot = segment_hot(starts, ends, base[0] + i * rows, rows)
     grad = summed[...].astype(F32)
-    grad_out[...] = grad
     accumulate(i == 0, grad_sq, col_sum(grad * grad))
     accumulate(i == 0, weight_sq, segment_sums(hot, master[...] * master[...]))
 
 
-def lamb_kernel(base, clip, starts, ends, grad, master, one, two, update_out, one_out, two_out, update_sq):
+def lamb_kernel(base, stats, starts, ends, summed, master, one, two, grad_out, update_out, one_out, two_out, update_sq):
     i = pl.program_id(0)
     rows = master.shape[0]
     hot = segment_hot(starts, ends, base[0] + i * rows, rows)
-    clipped = clip[0] * grad[...]
+    total_sq = jnp.sum(stats[0:1, :], axis=1, keepdims=True)
+    clip = jnp.minimum(1.0, clip_fraction * math.sqrt(NPARAM) / (jnp.sqrt(total_sq) + 1e-06))
+    grad = summed[...].astype(F32)
+    grad_out[...] = grad
+    clipped = clip * grad
     new_one = beta_one * one[...] + (1.0 - beta_one) * clipped
     new_two = beta_two * two[...] + (1.0 - beta_two) * clipped * clipped
     one_out[...] = new_one
@@ -389,6 +392,240 @@
     update = first_hat / (jnp.sqrt(second_hat) + adam_eps) + decay_rate * master[...]
     update_out[...] = update
     accumulate(i == 0, update_sq, segment_sums(hot, update * update))
+
+
+BATCH = 256
+HALF = 128
+QUARTER = 64
+MESH = pl.DeviceIdType.MESH
+
+
+class Place:
+    def __init__(self):
+        self.z = lax.axis_index("kf")
+        self.me = lax.axis_index("lat")
+        self.core = lax.rem(self.me, 2)
+        self.x = lax.rem(self.me // 2, 2)
+        self.y = self.me // 4
+        self.z_low = lax.rem(self.z, 2)
+        self.z_high = self.z // 2
+        self.sibling = (self.z, self.me + 1 - 2 * self.core)
+        self.x_side = (self.z, self.me + 2 - 4 * self.x)
+        self.y_side = (self.z, self.me + 4 - 8 * self.y)
+        self.z_near = (self.z + 1 - 2 * self.z_low, self.me)
+        self.z_far = (self.z + 2 - 4 * self.z_high, self.me)
+
+    def z_other(self, step):
+        return (lax.rem(self.z + step, 4), self.me)
+
+    def lat_other(self, step):
+        return (self.z, lax.rem(self.me + step, 8))
+
+
+def remote(src, dst, send, recv, device):
+    return pltpu.make_async_remote_copy(
+        src_ref=src, dst_ref=dst, send_sem=send, recv_sem=recv, device_id=device, device_id_type=MESH
+    )
+
+
+def greet(devices):
+    barrier = pltpu.get_barrier_semaphore()
+    for device in devices:
+        pl.semaphore_signal(barrier, inc=1, device_id=device, device_id_type=MESH)
+    pl.semaphore_wait(barrier, len(devices))
+
+
+def added(left, right):
+    return (left.astype(F32) + right.astype(F32)).astype(BF)
+
+
+class Reduction:
+    lags = (0, 1, 3, 5, 7, 9, 11)
+
+    def __init__(self, place, grads, out, bufs, sems):
+        self.p = place
+        self.grads = grads
+        self.out = out
+        self.own, self.rc, self.r1, self.r2, self.r3, self.r4, self.res = bufs
+        self.own_sem, self.send, self.rc_sem, self.r1_sem, self.r2_sem, self.r3_sem, self.r4_sem, self.res_sem = sems
+        self.shard = grads.shape[3]
+        self.batches = pl.cdiv(self.shard, BATCH)
+        self.back = self.batches * BATCH - self.shard
+
+    @staticmethod
+    def scratch(shard):
+        n = pl.cdiv(shard, BATCH)
+        bufs = [
+            pltpu.VMEM((2, 2, 2, BATCH, LANES), BF),
+            pltpu.VMEM((n, 2, 2, BATCH, LANES), BF),
+            pltpu.VMEM((n, 2, 2, HALF, LANES), BF),
+            pltpu.VMEM((n, 2, HALF, LANES), BF),
+            pltpu.VMEM((n, HALF, LANES), BF),
+            pltpu.VMEM((n, QUARTER, LANES), BF),
+            pltpu.VMEM((n, BATCH, LANES), BF),
+        ]
+        dma = pltpu.SemaphoreType.DMA
+        sems = [dma((2,)), dma((10, 4)), dma((n,)), dma((n, 2)), dma((n, 2)), dma((n,)), dma((n,)), dma((n, 3))]
+        return bufs + sems
+
+    def row(self, i):
+        return pl.multiple_of(i * BATCH - (i // (self.batches - 1)) * self.back, 16)
+
+    def own_copy(self, i):
+        slot = lax.rem(i, 2)
+        src = self.grads.at[:, :, self.p.core, pl.ds(self.row(i), BATCH), :]
+        return pltpu.make_async_copy(src, self.own.at[slot], self.own_sem.at[slot])
+
+    def copies(self, stage, i):
+        p, slot = self.p, lax.rem(i, 4)
+        if stage == 0:
+            src = self.grads.at[:, :, 1 - p.core, pl.ds(self.row(i), BATCH), :]
+            return [remote(src, self.rc.at[i], self.send.at[0, slot], self.rc_sem.at[i], p.sibling)]
+        if stage == 1:
+            to_x = self.rc.at[i, :, 1 - p.x, pl.ds(0, HALF), :]
+            to_y = self.rc.at[i, 1 - p.y, :, pl.ds(HALF, HALF), :]
+            return [
+                remote(to_x, self.r1.at[i, 0], self.send.at[1, slot], self.r1_sem.at[i, 0], p.x_side),
+                remote(to_y, self.r1.at[i, 1], self.send.at[2, slot], self.r1_sem.at[i, 1], p.y_side),
+            ]
+        if stage == 2:
+            to_y = self.r1.at[i, 0, 1 - p.y]
+            to_x = self.r1.at[i, 1, 1 - p.x]
+            return [
+                remote(to_y, self.r2.at[i, 0], self.send.at[3, slot], self.r2_sem.at[i, 0], p.y_side),
+                remote(to_x, self.r2.at[i, 1], self.send.at[4, slot], self.r2_sem.at[i, 1], p.x_side),
+            ]
+        if stage == 3:
+            src = self.r2.at[i, 1 - p.z_low]
+            return [remote(src, self.r3.at[i], self.send.at[5, slot], self.r3_sem.at[i], p.z_near)]
+        if stage == 4:
+            src = self.r3.at[i, pl.ds(pl.multiple_of((1 - p.z_high) * QUARTER, QUARTER), QUARTER), :]
+            return [remote(src, self.r4.at[i], self.send.at[6, slot], self.r4_sem.at[i], p.z_far)]
+        mine = self.res.at[i, pl.ds(pl.multiple_of(p.z_low * HALF + p.z_high * QUARTER, QUARTER), QUARTER), :]
+        return [
+            remote(mine, mine, self.send.at[6 + d, slot], self.res_sem.at[i, d - 1], p.z_other(d))
+            for d in (1, 2, 3)
+        ]
+
+    def launch(self, stage, i):
+        @pl.when(i >= 4)
+        def _():
+            for copy in self.copies(stage, i - 4):
+                copy.wait_send()
+
+        for copy in self.copies(stage, i):
+            copy.start()
+
+    def landed(self, stage, i):
+        for copy in self.copies(stage, i):
+            copy.wait_recv()
+
+    def work(self, stage, i):
+        p = self.p
+        if stage == 0:
+            self.own_copy(i).start()
+        elif stage == 1:
+            self.landed(0, i)
+            self.own_copy(i).wait()
+            self.rc[i] = added(self.rc[i], self.own[lax.rem(i, 2)])
+        elif stage == 2:
+            self.landed(1, i)
+            self.r1[i, 0] = added(self.r1[i, 0], self.rc[i, :, p.x, 0:HALF, :])
+            self.r1[i, 1] = added(self.r1[i, 1], self.rc[i, p.y, :, HALF:BATCH, :])
+        elif stage == 3:
+            self.landed(2, i)
+            self.r2[i, 0] = added(self.r2[i, 0], self.r1[i, 0, p.y])
+            self.r2[i, 1] = added(self.r2[i, 1], self.r1[i, 1, p.x])
+        elif stage == 4:
+            self.landed(3, i)
+            self.r3[i] = added(self.r3[i], self.r2[i, p.z_low])
+        elif stage == 5:
+            self.landed(4, i)
+            part = self.r3[i, pl.ds(pl.multiple_of(p.z_high * QUARTER, QUARTER), QUARTER), :]
+            at = pl.multiple_of(p.z_low * HALF + p.z_high * QUARTER, QUARTER)
+            self.res[i, pl.ds(at, QUARTER), :] = added(self.r4[i], part)
+        else:
+            self.landed(5, i)
+            self.out[pl.ds(self.row(i), BATCH), :] = self.res[i]
+        if stage < 6:
+            self.launch(stage, i)
+
+    def tick(self, t):
+        for stage, lag in enumerate(self.lags):
+            i = t - lag
+
+            @pl.when((i >= 0) & (i < self.batches))
+            def _(stage=stage, i=i):
+                self.work(stage, i)
+
+    def ticks(self):
+        return self.batches + self.lags[-1]
+
+    def finish(self):
+        for stage in range(6):
+            for back in range(4):
+                for copy in self.copies(stage, self.batches - 4 + back):
+                    copy.wait_send()
+
+    def partners(self):
+        p = self.p
+        return [p.sibling, p.x_side, p.y_side] + [p.z_other(d) for d in (1, 2, 3)]
+
+
+def share_all(place, block, send, recv):
+    mine = block.at[place.me]
+    copies = [
+        remote(mine, mine, send.at[d - 1], recv.at[d - 1], place.lat_other(d)) for d in range(1, 8)
+    ]
+    for copy in copies:
+        copy.start()
+    for copy in copies:
+        copy.wait()
+
+
+STAT_ROWS = 56
+
+
+def reduce_kernel(bias_owner, bias_at, starts, ends, grads, master, summed, stats, *scratch):
+    place = Place()
+    block, block_send, block_recv = scratch[:3]
+    red = Reduction(place, grads, summed, scratch[3:10], scratch[10:])
+    greet([place.lat_other(d) for d in range(1, 8)] + [place.z_other(d) for d in (1, 2, 3)])
+    lax.fori_loop(0, red.ticks(), lambda t, c: (red.tick(t), c)[1], 0)
+    shard = master.shape[0]
+    step = 784
+    grad_sq = jnp.zeros((1, LANES), F32)
+    weight_sq = jnp.zeros((16, LANES), F32)
+    for j in range(shard // step):
+        at = slice(j * step, (j + 1) * step)
+        part = summed[at, :].astype(F32)
+        grad_sq = grad_sq + col_sum(part * part)
+        hot = segment_hot(starts, ends, place.me * shard + j * step, step)
+        part = master[at, :]
+        weight_sq = weight_sq + segment_sums(hot, part * part)
+    bias = summed[bias_at : bias_at + 2 * FF // LANES, :].astype(F32)
+    bias = jnp.where(place.me == bias_owner, bias, 0.0)
+    head = jnp.concatenate([grad_sq, jnp.zeros((7, LANES), F32), weight_sq, bias], axis=0)
+    block[pl.ds(place.me, 1)] = head[None]
+    share_all(place, block, block_send, block_recv)
+    total = block[0]
+    for s in range(1, 8):
+        total = total + block[s]
+    stats[...] = total
+    red.finish()
+
+
+def trust_kernel(update_sq, stats, trust, block, send, recv):
+    place = Place()
+    greet([place.lat_other(d) for d in range(1, 8)])
+    block[pl.ds(place.me, 1)] = update_sq[...][None]
+    share_all(place, block, send, recv)
+    total = block[0]
+    for s in range(1, 8):
+        total = total + block[s]
+    update_norm = jnp.sqrt(jnp.sum(total, axis=1, keepdims=True))
+    weight_norm = jnp.sqrt(jnp.sum(stats[8:24, :], axis=1, keepdims=True))
+    trust[...] = jnp.broadcast_to(weight_norm / (update_norm + 1e-06), (16, LANES))
 
 
 def fixed(*shape):
@@ -427,6 +664,26 @@
         ),
         cost_estimate=pl.CostEstimate(flops=flops, bytes_accessed=moved, transcendentals=trans),
     )(*args)
+
+
+def reduce_all(local_flat, master_rows, starts, ends, bias_owner, bias_row):
+    shard = master_rows.shape[0]
+    vmem = pl.BlockSpec(memory_space=pltpu.VMEM)
+    block = [
+        pltpu.VMEM((8, STAT_ROWS, LANES), F32),
+        pltpu.SemaphoreType.DMA((7,)),
+        pltpu.SemaphoreType.DMA((7,)),
+    ]
+    return pl.pallas_call(
+        functools.partial(reduce_kernel, bias_owner, bias_row),
+        out_shape=[shaped((shard, LANES), BF), shaped((STAT_ROWS, LANES))],
+        in_specs=[vmem, vmem, pl.BlockSpec(memory_space=pl.ANY), vmem],
+        out_specs=[vmem, vmem],
+        scratch_shapes=block + Reduction.scratch(shard),
+        compiler_params=pltpu.CompilerParams(
+            collective_id=1, has_side_effects=True, vmem_limit_bytes=48 * MIB
+        ),
+    )(starts, ends, local_flat.reshape(2, 2, 2, shard, LANES), master_rows)
 
 
 def body(tokens, frame_ids, episodes, master, moment_one, moment_two, latent_grad):
@@ -637,9 +894,6 @@
     }
     layout = param_layout()
     local_flat = jnp.concatenate([grads[name].astype(BF).reshape(-1) for name, unused in layout])
-    summed = lax.psum_scatter(local_flat, "lat", scatter_dimension=0, tiled=True)
-    summed = lax.psum(summed, "kf")
-
     starts, ends, offset, bias_offset = [], [], 0, 0
     for name, shape in layout:
         if name == "hid_bias":
@@ -657,38 +911,54 @@
     smem = pl.BlockSpec(memory_space=pltpu.SMEM)
     flat_rows = (shard_rows, LANES)
     master_rows = master.reshape(flat_rows)
-    grad_shard, grad_sq, weight_sq = call(
-        grad_stats_kernel,
-        opt_steps,
-        [smem, fixed(16, LANES), fixed(16, LANES), rowed(opt_rows, LANES), rowed(opt_rows, LANES)],
-        [
-            (rowed(opt_rows, LANES), shaped(flat_rows)),
-            (kept(1, LANES), shaped((1, LANES))),
-            (kept(16, LANES), shaped((16, LANES))),
-        ],
-        (base, starts, ends, summed.reshape(flat_rows), master_rows),
-    )
     bias_owner, bias_at = divmod(bias_offset, shard_len)
-    bias_part = jnp.where(
-        lat_index == bias_owner, grad_shard.reshape(-1)[bias_at : bias_at + 2 * FF], 0.0
-    )
-    total_sq, weight_sq, bias_total = lax.psum(
-        (jnp.sum(grad_sq), jnp.sum(weight_sq, axis=1), bias_part), "lat"
-    )
-    bias_grad = bias_total.reshape(2, FF)
-    clip_scale = jnp.minimum(1.0, clip_fraction * math.sqrt(NPARAM) / (jnp.sqrt(total_sq) + 1e-06))
-    lamb_update, new_one, new_two, update_sq = call(
+    reach = lat_count == 8 and lax.axis_size("kf") == 4
+    if reach:
+        summed, stats = reduce_all(local_flat, master_rows, starts, ends, bias_owner, bias_at // LANES)
+    else:
+        summed = lax.psum_scatter(local_flat, "lat", scatter_dimension=0, tiled=True)
+        summed = lax.psum(summed, "kf").reshape(flat_rows)
+        grad_sq, weight_sq = call(
+            grad_stats_kernel,
+            opt_steps,
+            [smem, fixed(16, LANES), fixed(16, LANES), rowed(opt_rows, LANES), rowed(opt_rows, LANES)],
+            [(kept(1, LANES), shaped((1, LANES))), (kept(16, LANES), shaped((16, LANES)))],
+            (base, starts, ends, summed, master_rows),
+        )
+        bias_rows = summed[bias_at // LANES : bias_at // LANES + 2 * FF // LANES].astype(F32)
+        bias_rows = jnp.where(lat_index == bias_owner, bias_rows, 0.0)
+        stats = lax.psum(
+            jnp.concatenate([grad_sq, jnp.zeros((7, LANES), F32), weight_sq, bias_rows]), "lat"
+        )
+    bias_grad = stats[24:STAT_ROWS].reshape(2, FF)
+    grad_shard, lamb_update, new_one, new_two, update_sq = call(
         lamb_kernel,
         opt_steps,
-        [smem, smem, fixed(16, LANES), fixed(16, LANES)] + [rowed(opt_rows, LANES)] * 4,
-        [(rowed(opt_rows, LANES), shaped(flat_rows))] * 3 + [(kept(16, LANES), shaped((16, LANES)))],
+        [smem, fixed(STAT_ROWS, LANES), fixed(16, LANES), fixed(16, LANES)] + [rowed(opt_rows, LANES)] * 4,
+        [(rowed(opt_rows, LANES), shaped(flat_rows))] * 4 + [(kept(16, LANES), shaped((16, LANES)))],
         (
-            base, clip_scale.reshape(1), starts, ends, grad_shard, master_rows,
+            base, stats, starts, ends, summed, master_rows,
             moment_one.reshape(flat_rows), moment_two.reshape(flat_rows),
         ),
     )
-    update_sq = lax.psum(jnp.sum(update_sq, axis=1), "lat")
-    trust = (jnp.sqrt(weight_sq) / (jnp.sqrt(update_sq) + 1e-06))[: len(layout)]
+    if reach:
+        vmem = pl.BlockSpec(memory_space=pltpu.VMEM)
+        trust = pl.pallas_call(
+            trust_kernel,
+            out_shape=shaped((16, LANES)),
+            in_specs=[vmem, vmem],
+            out_specs=vmem,
+            scratch_shapes=[
+                pltpu.VMEM((8, 16, LANES), F32),
+                pltpu.SemaphoreType.DMA((7,)),
+                pltpu.SemaphoreType.DMA((7,)),
+            ],
+            compiler_params=pltpu.CompilerParams(collective_id=2, has_side_effects=True),
+        )(update_sq, stats)[: len(layout), 0]
+    else:
+        update_sq = lax.psum(jnp.sum(update_sq, axis=1), "lat")
+        weight_sq = jnp.sum(stats[8:24], axis=1)
+        trust = (jnp.sqrt(weight_sq) / (jnp.sqrt(update_sq) + 1e-06))[: len(layout)]
     return (
         latents_out,
         token_grad,

time: 722 us -> 539 us (0.75)
  waiting for transfers between devices: 254 us -> 42.6 us
  Pallas kernels: 208 us -> 284 us
  blocking collectives: 81.6 us -> 44.7 us
    unnamed x6 -> x3, waiting for transfers between devices: 156 us -> 0.05 us
    pallas_call x0 -> x2, Pallas kernels: none -> 82.1 us  [the longest x1 75.9 us: reduce_all(): pl.pallas_call(functools.partial(reduce_kernel, bias_owner, bias_row), ou...]
    psum x1 -> x0, waiting for transfers between devices: 56.4 us -> none  [body(): summed = lax.psum(summed, 'kf')]
    psum x2 -> x0, blocking collectives: 36.9 us -> none  [the longest x1 22.9 us: body(): update_sq = lax.psum(jnp.sum(update_sq, axis=1), 'lat')]
    pallas_call x9 -> x8, Pallas kernels: 208 us -> 202 us  [call(): pl.pallas_call(kernel, grid=(grid,), in_specs=in_specs, out_specs=list(ou...]
    unnamed x109 -> x94, local copies, waits for them, and re-layouts: 28.1 us -> 30.4 us
  transfers between devices with their start and end apart: 7 -> 5, of which waited for: 4 -> 2; matrix products, arithmetic and copies ran while one was open for 10% -> 16% of each run, Pallas kernels for 3% -> 18%
where the time goes in v2:
time: 539 us; the launch traced here: 535 us
  Pallas kernels  284 us (53%)
  local copies, waits for them, and re-layouts  78.4 us (15%)
  matrix products  46.9 us (9%)
  blocking collectives  44.7 us (8%)
  waiting for transfers between devices  42.6 us (8%)
  between operations  14.7 us (3%)
  other arithmetic  14.3 us (3%)
  starting transfers between devices  9.4 us (2%)
    pallas_call x8, Pallas kernels, call(): pl.pallas_call(kernel, grid=(grid,), in_specs=in_specs, out_specs=list(ou...  202 us
    pallas_call x1, Pallas kernels, reduce_all(): pl.pallas_call(functools.partial(reduce_kernel, bias_owner, bias_row), ou...  75.9 us
    all_gather x1, blocking collectives, body(): lax.all_gather(frame_ids[0].astype(BF), 'lat', axis=0, tiled=True)  44.7 us
    dot_general x7, matrix products, t_mm(): lax.dot_general(left, right, (((0,), (0,)), ((), ())), preferred_element_...  43.5 us
    unnamed x94, local copies, waits for them, and re-layouts  30.4 us
    all_gather x1, waiting for transfers between devices, body(): whole_flat = lax.all_gather(master.astype(BF), 'lat', axis=0, tiled=True)  29.2 us
    reduce_scatter x1, waiting for transfers between devices, body(): lax.psum_scatter(dkv_t.T.astype(BF), 'lat', scatter_dimension=0, tiled=True)  13.3 us
    slice x2, local copies, waits for them, and re-layouts, body(): weights['w_down'][1]  10.9 us
  transfers between devices with their start and end apart: 5, of which 2 were waited for; matrix products, arithmetic and copies ran while one was open for 16% of the time, Pallas kernels for 18%

profile of v2, /device:TPU:0, one launch (start us, length us, event | category | flops | bytes accessed | tf_op | source)
XLA Modules:
  0.0 535.4 jit_solution(4901165149290325228)
XLA Ops:
  7.2 3.0 convert_element_type.117
  10.3 5.3 all-to-all-start
  15.7 44.7 %all-gather = bf16[1,4096]{1,0:T(2,128)(2,1)S(1)} all-gather(bf16[1,512]{1,0:T(2,128)(2,1)S(1)} %convert_element_type.127), channel_id=2, replica_groups=mesh['kf'=4,'lat'=8] {'lat'}, dimensions={1}, use_global_device_ids=true | all-gather | bytes 9216 | tf_op jit(solution)/shard_map/all_gather | solution.py:711
  62.8 2.0 copy.31
  65.9 1.5 copy.28
  67.4 29.2 %all-gather.4.cloned.1.call-done = bf16[5619712]{0:T(1024)(128)(2,1)} async-done(((bf16[702464]{0:T(1024)(128)(2,1)}), bf16[5619712]{0:T(1024)(128)(2,1)}) %all-gather.4.cloned.1.call-update) | async-done | bytes 11239440 | tf_op jit(solution)/shard_map/all_gather | solution.py:704
  97.3 1.8 convolution_convert_fusion.6
  99.4 6.6 %fusion.30 = (bf16[1048576]{0:T(1024)(128)(2,1)}, bf16[1048576]{0:T(1024)(128)(2,1)}, bf16[1048576]{0:T(1024)(128)(2,1)}, bf16[1048576]{0:T(1024)(128)(2,1)}) fusion(bf16[5619712]{0:T(1024)(128)(2,1)} %all-gather.4.cloned.1.call-done), kind=kLoop, calls=%fused_computation.80 | loop fusion | bytes 16777216 | tf_op jit(solution)/shard_map/slice | solution.py:801
  105.9 3.1 copy-done.9
  117.1 2.7 reshape.358.w_qkv
  119.8 4.4 slice.253.w_down
  124.2 4.5 slice.246.w_down
  128.7 4.2 slice.244.w_up
  132.8 2.3 slice.251.w_up
  135.8 16.1 %shard_map.152 = (f32[2048,512]{1,0:T(8,128)}, bf16[4,512,128]{2,1,0:T(8,128)(2,1)}, bf16[2048,128]{1,0:T(8,128)(2,1)}, f32[4,1,512]{2,1,0:T(1,128)}) custom-call(bf16[512,512]{1,0:T(8,128)(2,1)} %slice.225.latent, f32[4,1,512]{2,1,0:T(1,128)} %reshape.356.episode, f32[8,512]{1,0:T(8,128)} %reshape.379.norms, bf16[512,128]{1,0:T(8,128)(2,1)} %pad.8.w_q, ...), custom_call_target="tpu_custom_call" | custom-call | flops 2684354560 | bytes 7200768 | tf_op jit(solution)/shard_map/pallas_call | solution.py:655
  151.9 31.0 %shard_map.153 = (f32[2048,512]{1,0:T(8,128)}, bf16[2048,512]{1,0:T(8,128)(2,1)}, bf16[2048,2048]{1,0:T(8,128)(2,1)}, bf16[2048,2048]{1,0:T(8,128)(2,1)}, bf16[2...) custom-call(f32[2048,512]{1,0:T(8,128)} %get-tuple-element.54.h1, f32[8,512]{1,0:T(8,128)} %reshape.379.norms, ...), custom_call_target="tpu_custom_call" | custom-call | flops 11811160064 | bytes 41459712 | tf_op jit(solution)/shard_map/pallas_call | solution.py:655
  182.9 22.7 %shard_map.154 = (f32[2048,512]{1,0:T(8,128)}, bf16[2048,512]{1,0:T(8,128)(2,1)}, f32[4,8,512]{2,1,0:T(8,128)}) custom-call(bf16[2048,1536]{1,0:T(8,128)(2,1)} %get-tuple-element.55.qkv, f32[2048,512]{1,0:T(8,128)} %get-tuple-element.56.h2, bf16[512,512]{1,0:T(8,128)(2,1)} %slice.249.w_so, f32[4,512]{1,0:T(4,128)} %reshape.380.out_bias), custom_call_target="tpu_custom_call" | custom-call | flops 8589934592 | bytes 17375232 | tf_op jit(solution)/shard_map/pallas_call | solution.py:655
  205.5 41.3 %shard_map.155 = (bf16[2048,512]{1,0:T(8,128)(2,1)}, f32[2048,512]{1,0:T(8,128)}, bf16[2048,512]{1,0:T(8,128)(2,1)}, bf16[2048,2048]{1,0:T(8,128)(2,1)}, bf16[20...) custom-call(f32[2048,512]{1,0:T(8,128)} %get-tuple-element.57.h3, ...), custom_call_target="tpu_custom_call" | custom-call | flops 17179869184 | bytes 35706880 | tf_op jit(solution)/shard_map/pallas_call | solution.py:655
  246.9 8.5 %fusion.3 = bf16[1,2048,512]{2,1,0:T(8,128)(2,1)S(1)} fusion(bf16[2048,2048]{1,0:T(8,128)(2,1)} %get-tuple-element.86, bf16[2048,512]{1,0:T(8,128)(2,1)S(1)} %bitcast.135), kind=kOutput, calls=%fused_computation.10 | convolution fusion | flops 4296015872 | bytes 12582912 | tf_op jit(solution)/shard_map/dot_general | solution.py:80
  255.4 36.3 %shard_map.156 = (f32[2048,512]{1,0:T(8,128)}, bf16[2048,512]{1,0:T(8,128)(2,1)}, bf16[2048,1536]{1,0:T(8,128)(2,1)}, f32[2,512]{1,0:T(2,128)}, f32[1,512]{1,0:T(1,128)}) custom-call(bf16[2048,1536]{1,0:T(8,128)(2,1)} %get-tuple-element.55.qkv, f32[4,8,512]{2,1,0:T(8,128)} %get-tuple-element.62.lse, f32[2048,512]{1,0:T(8,128)} %get-tuple-element.63.g3, ...), custom_call_target="tpu_custom_call" | custom-call | flops 21474836480 | bytes 29448192 | tf_op jit(solution)/shard_map/pallas_call | solution.py:655
  291.7 3.0 fusion.4
  294.9 7.3 %convolution_convert_fusion.4 = bf16[512,1536]{1,0:T(8,128)(2,1)} fusion(bf16[2048,512]{1,0:T(8,128)(2,1)S(1)} %copy-done.32, bf16[2048,1536]{1,0:T(8,128)(2,1)} %get-tuple-element.77), kind=kOutput, calls=%fused_computation.6 | convolution fusion | flops 3222011904 | bytes 9961472 | tf_op jit(solution)/shard_map/dot_general | solution.py:80
  302.2 4.3 reshape.368
  306.5 21.9 %shard_map.157 = (f32[2048,512]{1,0:T(8,128)}, bf16[2048,512]{1,0:T(8,128)(2,1)}, bf16[2048,2048]{1,0:T(8,128)(2,1)}, f32[2,512]{1,0:T(2,128)}, f32[1,2048]{1,0:T(1,128)}, /*index=5*/f32[1,512]{1,0:T(1,128)}) custom-call(f32[2048,512]{1,0:T(8,128)} %get-tuple-element.54.h1, f32[2048,512]{1,0:T(8,128)} %get-tuple-element.64.g2, ...), custom_call_target="tpu_custom_call" | custom-call | flops 8589934592 | bytes 35682304 | tf_op jit(solution)/shard_map/pallas_call | solution.py:655
  328.4 8.5 %fusion.2 = bf16[1,2048,512]{2,1,0:T(8,128)(2,1)S(1)} fusion(bf16[2048,2048]{1,0:T(8,128)(2,1)} %get-tuple-element.84, bf16[2048,512]{1,0:T(8,128)(2,1)} %get-tuple-element.85), kind=kOutput, calls=%fused_computation.9 | convolution fusion | flops 4296015872 | bytes 12582912 | tf_op jit(solution)/shard_map/dot_general | solution.py:80
  337.4 4.1 copy.39
  341.5 20.7 %shard_map.158 = (f32[512,512]{1,0:T(8,128)}, f32[4,1,512]{2,1,0:T(1,128)}, f32[2,512]{1,0:T(2,128)}, f32[512,128]{1,0:T(8,128)}, f32[128,512]{1,0:T(8,128)}, /*index=5*/f32[1,512]{1,0:T(1,128)}, f32[128,4096]{1,0:T(8,128)}) custom-call(bf16[512,512]{1,0:T(8,128)(2,1)} %slice.225.latent, f32[4,1,512]{2,1,0:T(1,128)} %reshape.356.episode, ...), custom_call_target="tpu_custom_call" | custom-call | flops 3489660928 | bytes 9828352 | tf_op jit(solution)/shard_map/pallas_call | solution.py:655
  362.3 2.8 convert_bitcast_fusion
  365.1 2.9 copy.29
  368.6 3.8 all-to-all-start.1
  374.1 1.5 convert_bitcast_fusion.2
  376.7 9.0 %fusion = bf16[1,512,2048]{2,1,0:T(8,128)(2,1)S(1)} fusion(bf16[2048,512]{1,0:T(8,128)(2,1)} %get-tuple-element.80, bf16[2048,2048]{1,0:T(8,128)(2,1)} %get-tuple-element.81), kind=kOutput, calls=%fused_computation.7 | convolution fusion | flops 4296015872 | bytes 12582912 | tf_op jit(solution)/shard_map/dot_general | solution.py:80
  385.7 4.9 fusion.1
  391.0 3.4 copy.38
  394.4 1.5 dynamic-update-slice.1
  395.9 13.3 %reduce-scatter.2.cloned.1.call-done = bf16[512,128]{0,1:T(8,128)(2,1)} async-done(((bf16[4096,128]{0,1:T(8,128)(2,1)}), bf16[512,128]{0,1:T(8,128)(2,1)}) %reduce-scatter.2.cloned.1.call-update) | async-done | bytes 131088 | tf_op jit(solution)/shard_map/reduce_scatter | solution.py:874
  409.2 1.3 fusion.16
  410.6 1.4 dynamic-update-slice.2
  412.6 2.3 fusion.6
  415.5 1.5 constant_dynamic-update-slice_fusion.6
  417.0 2.7 constant_dynamic-update-slice_fusion.5
  420.5 2.3 constant_dynamic-update-slice_fusion.3
  422.8 1.4 copy-done.7
  424.2 2.3 constant_dynamic-update-slice_fusion.2
  427.8 75.9 %shard_map.159 = (bf16[5488,128]{1,0:T(8,128)(2,1)S(1)}, f32[56,128]{1,0:T(8,128)S(1)}) custom-call(s32[16,128]{1,0:T(8,128)S(1)} %broadcast_in_dim.21.starts, s32[16,128]{1,0:T(8,128)S(1)} %broadcast_in_dim.22.ends, bf16[2,2,2,5488,128]{4,3,2,1,0:T(8,128)(2,1)} %bitcast.128, f32[5488,128]{1,0:T(8,128)S(1)} %bitcast.123), custom_call_target="tpu_custom_call" | custom-call | tf_op jit(solution)/shard_map/pallas_call | solution.py:677
  505.5 12.6 %shard_map.160 = (f32[5488,128]{1,0:T(8,128)}, f32[5488,128]{1,0:T(8,128)}, f32[5488,128]{1,0:T(8,128)}, f32[5488,128]{1,0:T(8,128)}, f32[16,128]{1,0:T(8,128)}) custom-call(s32[1]{0:T(128)} %bitcast.16.base, f32[56,128]{1,0:T(8,128)} %copy-done.4, s32[16,128]{1,0:T(8,128)} %copy-done.5, s32[16,128]{1,0:T(8,128)} %copy-done.6, bf16[5488,128]{1,0:T(8,128)(2,1)} %copy-done.3, ...), custom_call_target="tpu_custom_call" | custom-call | bytes 21127172 | tf_op jit(solution)/shard_map/pallas_call | solution.py:655
  518.1 6.2 %shard_map.161 = f32[16,128]{1,0:T(8,128)} custom-call(f32[16,128]{1,0:T(8,128)} %get-tuple-element.99.update_sq, f32[56,128]{1,0:T(8,128)} %copy-done.4), custom_call_target="tpu_custom_call" | custom-call | tf_op jit(solution)/shard_map/pallas_call | solution.py:946
  526.8 1.8 copy.30
  (164 shorter events, 25.2 us)
Async XLA Ops:
  7.2 57.6 %copy-start = (s32[1,32]{1,0:T(1,128)S(1)}, s32[1,32]{1,0:T(1,128)}, u32[]{:S(2)}) copy-start(s32[1,32]{1,0:T(1,128)} %param.11) | copy-start | bytes 388
  7.2 8.5 %copy-start.25 = (s32[1,512]{1,0:T(1,128)S(1)}, s32[1,512]{1,0:T(1,128)}, u32[]{:S(2)}) copy-start(s32[1,512]{1,0:T(1,128)} %param.10) | copy-start | bytes 6148
  7.2 89.4 %all-gather.4.cloned.1.call-start = ((), (), s32[]{:S(2)}) async-start(), calls=%async_computation.3 | async-start | bytes 12644352 | tf_op jit(solution)/shard_map/all_gather | solution.py:704
  10.3 54.5 %copy-start.11 = (bf16[1,512,256]{2,1,0:T(8,128)(2,1)S(1)}, bf16[1,512,256]{2,1,0:T(8,128)(2,1)}, u32[]{:S(2)}) copy-start(bf16[1,512,256]{2,1,0:T(8,128)(2,1)} %param.9) | copy-start | bytes 786436
  10.3 55.6 %all-to-all-start = ((bf16[32,64,512]{2,1,0:T(8,128)(2,1)}), bf16[32,64,512]{2,1,0:T(8,128)(2,1)S(1)}, u32[]{:S(2)}, u32[]{:S(2)}) async-start(bf16[32,64,512]{2,1,0:T(8,128)(2,1)} %bitcast.133), calls=%async_computation | async-start | bytes 4194304 | tf_op jit(solution)/shard_map/all_to_all | solution.py:700
  15.6 119.5 %all-gather.6.cloned.1.call-start = ((), (), s32[]{:S(2)}) async-start(), calls=%async_computation.4 | async-start | bytes 1179648 | tf_op jit(solution)/shard_map/all_gather | solution.py:722
  65.2 40.7 %copy-start.16 = (f32[512]{0:T(512)}, f32[512]{0:T(512)S(1)}, u32[]{:S(2)}) copy-start(f32[512]{0:T(512)S(1)} %fusion.17) | copy-start | bytes 6148
  99.1 10.6 %slice-start = ((bf16[5619712]{0:T(1024)(128)(2,1)}), bf16[5632]{0:T(1024)(128)(2,1)S(1)}, s32[]{:S(2)}) async-start(bf16[5619712]{0:T(1024)(128)(2,1)} %all-gather.4.cloned.1.call-done), calls=%async_computation.6 | async-start | bytes 24576 | tf_op jit(solution)/shard_map/slice | solution.py:59
  99.1 310.1 %reduce-scatter.2.cloned.1.call-start = ((), (), s32[]{:S(2)}) async-start(), calls=%async_computation.5 | async-start | bytes 1179648 | tf_op jit(solution)/shard_map/reduce_scatter | solution.py:874
  99.4 9.7 %copy-start.9 = (bf16[5619712]{0:T(1024)(128)(2,1)S(1)}, bf16[5619712]{0:T(1024)(128)(2,1)}, u32[]{:S(2)}) copy-start(bf16[5619712]{0:T(1024)(128)(2,1)} %all-gather.4.cloned.1.call-done) | copy-start | bytes 33718276
  109.0 8.1 %slice-start.1 = ((bf16[5619712]{0:T(1024)(128)(2,1)}), bf16[786432]{0:T(1024)(128)(2,1)S(1)}, s32[]{:S(2)}) async-start(bf16[5619712]{0:T(1024)(128)(2,1)} %all-gather.4.cloned.1.call-done), calls=%async_computation.7 | async-start | bytes 3145728 | tf_op jit(solution)/shard_map/slice | solution.py:59
  124.2 8.6 %copy-start.10 = (bf16[1048576]{0:T(1024)(128)(2,1)S(1)}, bf16[1048576]{0:T(1024)(128)(2,1)}, u32[]{:S(2)}) copy-start(bf16[1048576]{0:T(1024)(128)(2,1)} %get-tuple-element.108) | copy-start | bytes 6291460
  205.5 41.3 %copy-start.12 = (bf16[8,4,64,512]{3,2,0,1:T(8,128)(2,1)S(1)}, bf16[8,4,64,512]{3,2,0,1:T(8,128)(2,1)}, u32[]{:S(2)}) copy-start(bf16[8,4,64,512]{3,2,0,1:T(8,128)(2,1)} %copy.28) | copy-start | bytes 6291460
  255.4 36.3 %copy-start.14 = (bf16[2048,512]{1,0:T(8,128)(2,1)S(1)}, bf16[2048,512]{1,0:T(8,128)(2,1)}, u32[]{:S(2)}) copy-start(bf16[2048,512]{1,0:T(8,128)(2,1)} %get-tuple-element.78) | copy-start | bytes 6291460
  291.6 3.3 copy-start.32
  362.2 2.9 copy-start.13
  362.2 5.9 %copy-start.24 = (f32[2,512]{1,0:T(2,128)S(1)}, f32[2,512]{1,0:T(2,128)}, u32[]{:S(2)}) copy-start(f32[2,512]{1,0:T(2,128)} %get-tuple-element.70) | copy-start | bytes 12292
  362.2 5.9 %copy-start.29 = (f32[1,512]{1,0:T(1,128)S(1)}, f32[1,512]{1,0:T(1,128)}, u32[]{:S(2)}) copy-start(f32[1,512]{1,0:T(1,128)} %get-tuple-element.89) | copy-start | bytes 6148
  362.2 5.9 %copy-start.23 = (f32[2,512]{1,0:T(2,128)S(1)}, f32[2,512]{1,0:T(2,128)}, u32[]{:S(2)}) copy-start(f32[2,512]{1,0:T(2,128)} %get-tuple-element.71) | copy-start | bytes 12292
  362.2 5.9 %copy-start.28 = (f32[1,512]{1,0:T(1,128)S(1)}, f32[1,512]{1,0:T(1,128)}, u32[]{:S(2)}) copy-start(f32[1,512]{1,0:T(1,128)} %get-tuple-element.90) | copy-start | bytes 6148
  362.2 5.9 %copy-start.22 = (f32[2,512]{1,0:T(2,128)S(1)}, f32[2,512]{1,0:T(2,128)}, u32[]{:S(2)}) copy-start(f32[2,512]{1,0:T(2,128)} %get-tuple-element.72) | copy-start | bytes 12292
  362.2 6.0 %copy-start.27 = (f32[1,512]{1,0:T(1,128)S(1)}, f32[1,512]{1,0:T(1,128)}, u32[]{:S(2)}) copy-start(f32[1,512]{1,0:T(1,128)} %get-tuple-element.91) | copy-start | bytes 6148
  362.2 6.0 %copy-start.21 = (f32[2,512]{1,0:T(2,128)S(1)}, f32[2,512]{1,0:T(2,128)}, u32[]{:S(2)}) copy-start(f32[2,512]{1,0:T(2,128)} %get-tuple-element.73) | copy-start | bytes 12292
  362.2 6.0 %copy-start.26 = (f32[1,512]{1,0:T(1,128)S(1)}, f32[1,512]{1,0:T(1,128)}, u32[]{:S(2)}) copy-start(f32[1,512]{1,0:T(1,128)} %get-tuple-element.92) | copy-start | bytes 6148
  362.3 6.1 %copy-start.20 = (f32[4,1,512]{2,1,0:T(1,128)S(1)}, f32[4,1,512]{2,1,0:T(1,128)}, u32[]{:S(2)}) copy-start(f32[4,1,512]{2,1,0:T(1,128)} %get-tuple-element.69) | copy-start | bytes 24580
  362.3 6.3 %copy-start.19 = (f32[1,2048]{1,0:T(1,128)S(1)}, f32[1,2048]{1,0:T(1,128)}, u32[]{:S(2)}) copy-start(f32[1,2048]{1,0:T(1,128)} %get-tuple-element.87) | copy-start | bytes 24580
  362.3 6.3 %copy-start.18 = (f32[1,2048]{1,0:T(1,128)S(1)}, f32[1,2048]{1,0:T(1,128)}, u32[]{:S(2)}) copy-start(f32[1,2048]{1,0:T(1,128)} %get-tuple-element.88) | copy-start | bytes 24580
  365.1 8.9 %copy-start.15 = (f32[512,128]{1,0:T(8,128)S(1)}, f32[512,128]{1,0:T(8,128)}, u32[]{:S(2)}) copy-start(f32[512,128]{1,0:T(8,128)} %get-tuple-element.74) | copy-start | bytes 786436
  368.6 158.2 %all-to-all-start.1 = ((bf16[4,512,512]{2,0,1:T(4,128)(2,1)}), bf16[4,512,512]{2,0,1:T(4,128)(2,1)S(1)}, u32[]{:S(2)}, u32[]{:S(2)}) async-start(bf16[4,512,512]{2,0,1:T(4,128)(2,1)} %copy.29), calls=%async_computation.1 | async-start | bytes 4194304 | tf_op jit(solution)/shard_map/all_to_all | solution.py:806
  374.1 11.5 %slice-start.2 = ((s8[8388608]{0:T(1024)(128)(4,1)}), s8[4194304]{0:T(1024)(128)(4,1)S(1)}, s32[]{:S(2)}) async-start(s8[8388608]{0:T(1024)(128)(4,1)} %bitcast.154), calls=%async_computation.8 | async-start | bytes 8388608
  376.7 9.0 %slice-start.3 = ((s8[8388608]{0:T(1024)(128)(4,1)}), s8[4194304]{0:T(1024)(128)(4,1)S(1)}, s32[]{:S(2)}) async-start(s8[8388608]{0:T(1024)(128)(4,1)} %bitcast.154), calls=%async_computation.9 | async-start | bytes 8388608
  376.7 9.0 %copy-start.33 = (bf16[2048,512]{1,0:T(8,128)(2,1)S(1)}, bf16[2048,512]{1,0:T(8,128)(2,1)}, u32[]{:S(2)}) copy-start(bf16[2048,512]{1,0:T(8,128)(2,1)} %get-tuple-element.82) | copy-start | bytes 6291460
  412.0 8.5 %copy-start.8 = (bf16[128,16,8,128]{3,1,2,0:T(8,128)(2,1)S(1)}, bf16[128,16,8,128]{3,1,2,0:T(8,128)(2,1)}, u32[]{:S(2)}) copy-start(bf16[128,16,8,128]{3,1,2,0:T(8,128)(2,1)} %copy.38) | copy-start | bytes 12582916
  420.5 3.7 copy-start.7
  424.2 3.5 copy-start.31
  424.2 3.5 copy-start.30
  424.2 3.6 copy-start.2
  427.8 76.0 %copy-start.5 = (s32[16,128]{1,0:T(8,128)}, s32[16,128]{1,0:T(8,128)S(1)}, u32[]{:S(2)}) copy-start(s32[16,128]{1,0:T(8,128)S(1)} %broadcast_in_dim.21.starts) | copy-start | bytes 24580
  427.8 75.9 %copy-start.6 = (s32[16,128]{1,0:T(8,128)}, s32[16,128]{1,0:T(8,128)S(1)}, u32[]{:S(2)}) copy-start(s32[16,128]{1,0:T(8,128)S(1)} %broadcast_in_dim.22.ends) | copy-start | bytes 24580
  503.8 1.1 copy-start.3
  504.9 0.6 copy-start.4
  505.5 20.1 %copy-start.17 = (f32[512]{0:T(512)S(1)}, f32[512]{0:T(512)}, u32[]{:S(2)}) copy-start(f32[512]{0:T(512)} %copy-done.16) | copy-start | bytes 6148
  505.5 23.1 %copy-start.1 = (s32[1,32]{1,0:T(1,128)S(1)}, s32[1,32]{1,0:T(1,128)}, u32[]{:S(2)}) copy-start(s32[1,32]{1,0:T(1,128)} %param.11) | copy-start | bytes 388
Sparse Core Ops, SparseCore 0:
  10.5 86.0 all-gather.3
  99.2 23.4 all-gather.5
  368.2 40.9 reduce-scatter.1
